TPU v7x, 32 devices: a whole 2x2x4 slice. The times are simulated.
32 devices in a mesh: doc: 4 (over y, x), seq: 8 (over z, core).
Axes of the slice: x: 2, y: 2, z: 4, core: 2. Of those that a mesh axis runs over, the one named last changes fastest.
Arguments:
- hidden_in: bfloat16 [4, 4096, 2048], P('doc', 'seq'), may hold values from -6 to 6
- cotangent: bfloat16 [4, 4096, 2048], P('doc', 'seq'), may hold values from -6 to 6
- scan_init: float32 [4, 16, 4096], P('doc'), may hold values from -4 to 4
- conv_init: bfloat16 [4, 3, 4096], P('doc'), may hold values from -6 to 6
- norm_gain: bfloat16 [2048], P('seq'), may hold values from 0.5 to 1.5
- in_weight: bfloat16 [2048, 8192], P('seq'), may hold values from -0.125 to 0.125
- conv_weight: bfloat16 [4, 4096], P(None, 'seq'), may hold values from -3 to 3
- conv_bias: bfloat16 [4096], P('seq'), may hold values from -1.5 to 1.5
- xproj_weight: bfloat16 [4096, 160], P('seq'), may hold values from -0.09375 to 0.09375
- dt_weight: bfloat16 [128, 4096], P(None, 'seq'), may hold values from -0.5 to 0.5
- dt_bias: bfloat16 [4096], P('seq'), may hold values from -3.5 to -2.5
- a_log: bfloat16 [16, 4096], P(None, 'seq'), may hold values from -8.7 to 2.1
- skip_d: bfloat16 [4096], P('seq'), may hold values from 0.5 to 1.5
- out_weight: bfloat16 [2048, 4096], P('seq'), may hold values from -0.1875 to 0.1875
Outputs:
- output: bfloat16 [4, 4096, 2048], P('doc', 'seq')
- input_grad: float32 [4, 4096, 2048], P('doc', 'seq')
- scan_init_grad: float32 [4, 16, 4096], P('doc')
- conv_init_grad: float32 [4, 3, 4096], P('doc')
- norm_gain_grad: float32 [2048], P('seq')
- in_weight_grad: float32 [2048, 8192], P('seq')
- conv_weight_grad: float32 [4, 4096], P(None, 'seq')
- conv_bias_grad: float32 [4096], P('seq')
- xproj_weight_grad: float32 [4096, 160], P('seq')
- dt_weight_grad: float32 [128, 4096], P(None, 'seq')
- dt_bias_grad: float32 [4096], P('seq')
- a_log_grad: float32 [16, 4096], P(None, 'seq')
- skip_d_grad: float32 [4096], P('seq')
- out_weight_grad: float32 [2048, 4096], P('seq')
All inputs are finite; a program needn't handle non-finite values.
Results may differ from a plain program's by a relative error of at most 0.014.
Values may be sent and summed in bfloat16 or wider, within the bound.
No kernel may reach another device: no remote copies, remote signals or barrier semaphores. Data moves between devices by JAX's collectives and lax.ppermute only.
A program may use at most 448 MiB of HBM per device.

v0:
```python
import jax
import jax.numpy as jnp
from jax import lax
from jax.sharding import PartitionSpec as P

SCAN_BLOCK = 32


NORM_EPS = 1e-05
CONTRACT_LAST = (((1,), (1,)), ((), ()))
CONTRACT_FIRST = (((0,), (0,)), ((), ()))


def shifted(block, axis, distance):
    devices = range(lax.axis_size(axis))
    route = [(i - distance, i) for i in devices if i - distance in devices]
    return lax.ppermute(block, axis, route)


def entering(x, axis, combine, identity):
    peers, mine = (lax.axis_size(axis), lax.axis_index(axis))
    everything = jax.tree.map(
        lambda part, kind: lax.all_gather(part.astype(kind), axis), x, (jnp.bfloat16, jnp.bfloat16)
    )
    start = jax.tree.map(
        lambda part, zero: jnp.broadcast_to(jnp.asarray(zero, part.dtype), part.shape), x, identity
    )

    def entering_step(k, before):
        reached = k < mine
        new = combine(
            before, jax.tree.map(lambda part, own: part[k].astype(own.dtype), everything, x)
        )
        return jax.tree.map(lambda a, b: jnp.where(reached, a, b), new, before)

    return lax.fori_loop(0, peers, entering_step, start)


def prefix(x, axis, combine, identity):
    peers, mine = (lax.axis_size(axis), lax.axis_index(axis))
    everything = jax.tree.map(
        lambda part, kind: lax.all_gather(part.astype(kind), axis),
        x,
        jax.tree.map(lambda a: jnp.bfloat16 if a.dtype == jnp.float32 else a.dtype, x),
    )
    start = jax.tree.map(
        lambda part, zero: jnp.broadcast_to(jnp.asarray(zero, part.dtype), part.shape), x, identity
    )

    def prefix_step(k, before):
        at = peers - 1 - k
        reached = at > mine
        new = combine(
            before, jax.tree.map(lambda part, own: part[at].astype(own.dtype), everything, x)
        )
        return jax.tree.map(lambda a, b: jnp.where(reached, a, b), new, before)

    return lax.fori_loop(0, peers, prefix_step, start)


def scan_block(state_now, blk_rows, neg_rate):
    outputs = []
    for position in range(blk_rows[0].shape[0]):
        decay_now = jnp.exp(blk_rows[0][position][None, :] * neg_rate)
        state_now = (
            decay_now * state_now + blk_rows[2][position][:, None] * blk_rows[1][position][None, :]
        )
        if len(blk_rows) == 4:
            outputs.append(jnp.sum(blk_rows[3][position][:, None] * state_now, axis=0))
    if len(blk_rows) == 4:
        return (state_now, jnp.stack(outputs))
    return (state_now, None)


def run_blocks(state_now, inputs, neg_rate):
    blocks = inputs[0].shape[0] // SCAN_BLOCK
    blocked = tuple((value.reshape((blocks, SCAN_BLOCK) + value.shape[1:]) for value in inputs))

    def block_step(carry_in, blk_rows):
        return scan_block(carry_in, blk_rows, neg_rate)

    final_state, outputs = lax.scan(jax.checkpoint(block_step), state_now, blocked)
    if outputs is None:
        return (final_state, None)
    return (final_state, outputs.reshape(inputs[0].shape))


def silu_slope(values):
    sigma = jax.nn.sigmoid(values)
    return sigma * (1.0 + values * (1.0 - sigma))


def chain_join(earlier, later):
    return (earlier[0] * later[0], later[0] * earlier[1] + later[1])


def shift_rim(inner_x, conv_state, is_first):
    lead_rows = conv_state.shape[0]
    tail_rows = inner_x[inner_x.shape[0] - lead_rows :]
    arrived = shifted(tail_rows.astype(jnp.bfloat16), "seq", 1).astype(tail_rows.dtype)
    return jnp.where(is_first, conv_state, arrived)


def carry_prefix(decay_all, end_state, start_state):
    before, carried = entering(
        (decay_all, end_state),
        "seq",
        chain_join,
        (jnp.ones_like(decay_all), jnp.zeros_like(end_state)),
    )
    return (before, before * start_state + carried)


def shards(
    hidden_in,
    cotangent,
    scan_init,
    conv_init,
    norm_gain,
    in_weight,
    conv_weight,
    conv_bias,
    xproj_weight,
    dt_weight,
    dt_bias,
    a_log,
    skip_d,
    out_weight,
):
    residual = hidden_in[0].astype(jnp.float32)
    cot_rows = cotangent[0]
    start_state = scan_init[0]
    conv_state = conv_init[0].astype(jnp.float32)
    tokens = residual.shape[0]
    model_width = residual.shape[1]
    inner_width = in_weight.shape[1] // 2
    rank_width = dt_weight.shape[0]
    state_count = a_log.shape[0]
    lead_rows = conv_state.shape[0]
    is_first = lax.axis_index("seq") == 0
    inv_scale = lax.rsqrt(jnp.mean(residual * residual, axis=1, keepdims=True) + NORM_EPS)
    scaled = residual * inv_scale
    rows_in = lax.all_gather(in_weight, "seq", axis=0, tiled=True)
    gain_rows = lax.all_gather(norm_gain, "seq", axis=0, tiled=True)
    gain_wide = gain_rows.astype(jnp.float32)
    normed_part = (scaled * gain_wide).astype(jnp.bfloat16)
    projected = jnp.dot(normed_part, rows_in, preferred_element_type=jnp.float32)
    gain_full = gain_wide
    front_out = (projected, normed_part, gain_full)
    projected = front_out[0]
    normed = front_out[1]
    gain_full = front_out[2]
    conv_taps, conv_shift, xproj_full, dt_full, dt_shift, rate_log, skip_full = (
        lax.all_gather(conv_weight, "seq", axis=1, tiled=True),
        lax.all_gather(conv_bias, "seq", axis=0, tiled=True),
        lax.all_gather(xproj_weight, "seq", axis=0, tiled=True),
        lax.all_gather(dt_weight, "seq", axis=1, tiled=True),
        lax.all_gather(dt_bias, "seq", axis=0, tiled=True),
        lax.all_gather(a_log, "seq", axis=1, tiled=True),
        lax.all_gather(skip_d, "seq", axis=0, tiled=True),
    )
    conv_taps = conv_taps.astype(jnp.float32)
    conv_shift = conv_shift.astype(jnp.float32)
    dt_shift = dt_shift.astype(jnp.float32)
    skip_full = skip_full.astype(jnp.float32)
    neg_rate = -jnp.exp(rate_log.astype(jnp.float32))
    tap_count = conv_taps.shape[0]
    inner_x = projected[:, :inner_width]
    gate_in = projected[:, inner_width:]
    rim_rows = shift_rim(inner_x, conv_state, is_first)
    extended = jnp.concatenate([rim_rows, inner_x], axis=0)
    conv_pre = conv_shift + conv_taps[0] * extended[:tokens]
    for offset in range(1, tap_count):
        conv_pre = conv_pre + conv_taps[offset] * extended[offset : offset + tokens]
    mixed = jax.nn.silu(conv_pre).astype(jnp.bfloat16)
    mixed_wide = mixed.astype(jnp.float32)
    xdbl_rows = jnp.dot(mixed, xproj_full, preferred_element_type=jnp.float32)
    rank_in = xdbl_rows[:, :rank_width].astype(jnp.bfloat16)
    b_rows = xdbl_rows[:, rank_width : rank_width + state_count]
    c_rows = xdbl_rows[:, rank_width + state_count :]
    dt_pre = jnp.dot(rank_in, dt_full, preferred_element_type=jnp.float32) + dt_shift
    step_size = jax.nn.softplus(dt_pre)
    drive_in = step_size * mixed_wide

    def end_part(step_size, drive_in, b_rows, neg_rate):
        final_state = run_blocks(jnp.zeros_like(neg_rate), (step_size, drive_in, b_rows), neg_rate)[
            0
        ]
        return (final_state, jnp.exp(neg_rate * jnp.sum(step_size, axis=0)))

    (end_state, decay_all), end_back = jax.vjp(end_part, step_size, drive_in, b_rows, neg_rate)
    before, start_here = carry_prefix(decay_all, end_state, start_state)

    def scan_part(state_now, step_size, drive_in, b_rows, c_rows, neg_rate):
        return run_blocks(state_now, (step_size, drive_in, b_rows, c_rows), neg_rate)[1]

    scanned, scan_back = jax.vjp(
        scan_part, start_here, step_size, drive_in, b_rows, c_rows, neg_rate
    )
    y_total = scanned + skip_full * mixed_wide
    gate_act = jax.nn.silu(gate_in)
    gated_out = (y_total * gate_act).astype(jnp.bfloat16)
    piece = lax.all_gather(out_weight, "seq", axis=0, tiled=True)
    columns = lax.dot_general(gated_out, piece, CONTRACT_LAST, preferred_element_type=jnp.float32)
    branch_part = lax.dynamic_update_slice_in_dim(
        (
            jnp.zeros((tokens, model_width), jnp.float32),
            jnp.zeros((tokens, inner_width), jnp.float32),
        )[0],
        columns,
        jnp.int32(0),
        1,
    )
    d_gated = jnp.dot(cot_rows, piece, preferred_element_type=jnp.float32)
    output = (residual + branch_part).astype(jnp.bfloat16)
    d_y = d_gated * gate_act
    d_gate_in = d_gated * y_total * silu_slope(gate_in)
    skip_grad = jnp.sum(d_y * mixed_wide, axis=0)
    d_mixed = d_y * skip_full
    d_start, d_step, d_drive, d_in, d_out, d_rate = scan_back(d_y)
    rim_back = shift_rim(inner_x, conv_state, is_first)
    before_back, start_back = carry_prefix(decay_all, end_state, start_state)
    later_sum = prefix(
        (decay_all, d_start), "seq", chain_join, (jnp.ones_like(decay_all), jnp.zeros_like(d_start))
    )[1]
    end_step, end_drive, end_in, end_rate = end_back((later_sum, later_sum * start_back))
    d_drive = d_drive + end_drive
    d_step = d_step + end_step + d_drive * mixed_wide
    d_mixed = d_mixed + d_drive * step_size
    d_in = d_in + end_in
    rate_grad = (d_rate + end_rate) * neg_rate
    d_pre = d_step * jax.nn.sigmoid(dt_pre)
    dt_bias_grad = jnp.sum(d_pre, axis=0)
    d_pre_low = d_pre.astype(jnp.bfloat16)
    dt_weight_grad = lax.dot_general(
        rank_in, d_pre_low, CONTRACT_FIRST, preferred_element_type=jnp.float32
    )
    d_rank = lax.dot_general(d_pre_low, dt_full, CONTRACT_LAST, preferred_element_type=jnp.float32)
    d_proj = jnp.concatenate([d_rank, d_in, d_out], axis=1).astype(jnp.bfloat16)
    xproj_grad = lax.dot_general(mixed, d_proj, CONTRACT_FIRST, preferred_element_type=jnp.float32)
    d_mixed = d_mixed + lax.dot_general(
        d_proj, xproj_full, CONTRACT_LAST, preferred_element_type=jnp.float32
    )
    d_conv = d_mixed * silu_slope(conv_pre)
    conv_bias_grad = jnp.sum(d_conv, axis=0)
    extended_back = jnp.concatenate([rim_back, inner_x], axis=0)
    conv_weight_grad = jnp.stack(
        [
            jnp.sum(d_conv * extended_back[offset : offset + tokens], axis=0)
            for offset in range(tap_count)
        ]
    )
    d_ext = jnp.pad(conv_taps[0] * d_conv, ((0, lead_rows), (0, 0)))
    for offset in range(1, tap_count):
        d_ext = d_ext + jnp.pad(conv_taps[offset] * d_conv, ((offset, lead_rows - offset), (0, 0)))
    passed_back = shifted(d_ext[:lead_rows].astype(jnp.bfloat16), "seq", -1).astype(jnp.float32)
    d_inner = d_ext[lead_rows:] + jnp.pad(passed_back, ((tokens - lead_rows, 0), (0, 0)))
    conv_init_part = jnp.where(is_first, d_ext[:lead_rows], 0.0)
    d_both = jnp.concatenate([d_inner, d_gate_in], axis=1).astype(jnp.bfloat16)
    d_normed = lax.dot_general(
        d_both,
        lax.all_gather(in_weight, "seq", axis=0, tiled=True),
        CONTRACT_LAST,
        preferred_element_type=jnp.float32,
    )
    gain_grad = jnp.sum(d_normed * scaled, axis=0)
    gain_part = d_normed * gain_full
    input_grad = cot_rows.astype(jnp.float32) + inv_scale * (
        gain_part - scaled * jnp.mean(gain_part * scaled, axis=1, keepdims=True)
    )
    gain_sum, conv_w_sum, conv_b_sum, xproj_sum, dt_w_sum, dt_b_sum, rate_sum, skip_sum = (
        lax.psum_scatter(gain_grad, "seq", scatter_dimension=0, tiled=True),
        lax.psum_scatter(conv_weight_grad, "seq", scatter_dimension=1, tiled=True),
        lax.psum_scatter(conv_bias_grad, "seq", scatter_dimension=0, tiled=True),
        lax.psum_scatter(xproj_grad, "seq", scatter_dimension=0, tiled=True),
        lax.psum_scatter(dt_weight_grad, "seq", scatter_dimension=1, tiled=True),
        lax.psum_scatter(dt_bias_grad, "seq", scatter_dimension=0, tiled=True),
        lax.psum_scatter(rate_grad, "seq", scatter_dimension=1, tiled=True),
        lax.psum_scatter(skip_grad, "seq", scatter_dimension=0, tiled=True),
    )
    state_grad, conv_grad = lax.psum((before_back * d_start, conv_init_part), "seq")
    doc_count = lax.axis_size("doc")
    seq_count = lax.axis_size("seq")
    piece_rows = in_weight.shape[0] // doc_count
    logical = jnp.arange(piece_rows * lax.axis_size(("doc", "seq")), dtype=jnp.int32)
    block_id = logical // piece_rows
    doc_pos = block_id // seq_count
    seq_pos = block_id % seq_count
    real_rows = (seq_pos * doc_count + doc_pos) * piece_rows + logical % piece_rows
    left_rows = jnp.take(normed, real_rows, axis=1)
    right_rows = jnp.take(cot_rows, real_rows, axis=1)
    in_part = lax.dot_general(left_rows, d_both, CONTRACT_FIRST, preferred_element_type=jnp.float32)
    out_part = lax.dot_general(
        right_rows, gated_out, CONTRACT_FIRST, preferred_element_type=jnp.float32
    )
    joint_sums = lax.psum_scatter(
        jnp.concatenate([in_part, out_part], axis=1),
        ("doc", "seq"),
        scatter_dimension=0,
        tiled=True,
    )
    matrix_sums = lax.all_gather(joint_sums.astype(jnp.bfloat16), "doc", axis=0, tiled=True).astype(
        joint_sums.dtype
    )
    in_total = matrix_sums[:, : 2 * inner_width]
    out_total = matrix_sums[:, 2 * inner_width :]
    small_total = (
        lax.psum(gain_sum.astype(jnp.bfloat16), "doc").astype(jnp.float32),
        lax.psum(conv_w_sum.astype(jnp.bfloat16), "doc").astype(jnp.float32),
        lax.psum(conv_b_sum.astype(jnp.bfloat16), "doc").astype(jnp.float32),
        lax.psum(xproj_sum.astype(jnp.bfloat16), "doc").astype(jnp.float32),
        lax.psum(dt_w_sum.astype(jnp.bfloat16), "doc").astype(jnp.float32),
        lax.psum(dt_b_sum.astype(jnp.bfloat16), "doc").astype(jnp.float32),
        lax.psum(rate_sum.astype(jnp.bfloat16), "doc").astype(jnp.float32),
        lax.psum(skip_sum.astype(jnp.bfloat16), "doc").astype(jnp.float32),
    )
    return (
        output[None],
        input_grad[None],
        state_grad[None],
        conv_grad[None],
        small_total[0],
        in_total,
        small_total[1],
        small_total[2],
        small_total[3],
        small_total[4],
        small_total[5],
        small_total[6],
        small_total[7],
        out_total,
    )


def solution(mesh):
    placed = (
        P("doc", "seq", None),
        P("doc", "seq", None),
        P("doc", None, None),
        P("doc", None, None),
        P("seq"),
        P("seq", None),
        P(None, "seq"),
        P("seq"),
        P("seq", None),
        P(None, "seq"),
        P("seq"),
        P(None, "seq"),
        P("seq"),
        P("seq", None),
    )
    return jax.shard_map(
        shards,
        mesh=mesh,
        in_specs=placed,
        out_specs=(
            P("doc", "seq", None),
            P("doc", "seq", None),
            P("doc", None, None),
            P("doc", None, None),
            P("seq"),
            P("seq", None),
            P(None, "seq"),
            P("seq"),
            P("seq", None),
            P(None, "seq"),
            P("seq"),
            P(None, "seq"),
            P("seq"),
            P("seq", None),
        ),
        check_vma=False,
    )
```

profile of v0, /device:TPU:0, one launch (start us, length us, event | category | flops | bytes accessed | tf_op | source)
XLA Modules:
  0.0 3722.5 jit_solution(10681707176558629973)
XLA Ops:
  26.3 27.9 all_gather.60
  56.2 245.0 %all-gather.16.cloned.1.call-done = bf16[2048,8192]{1,0:T(8,128)(2,1)} async-done(((bf16[256,8192]{1,0:T(8,128)(2,1)}), bf16[2048,8192]{1,0:T(8,128)(2,1)}) %all-gather.16.cloned.1.call-update) | async-done | bytes 33554448 | tf_op jit(solution)/shard_map/all_gather | solution.py:143
  301.2 27.3 fusion.224
  331.5 19.3 all_gather.58
  364.2 19.2 all-gather.3
  391.6 61.9 %all-gather.22.cloned.1.call-done = bf16[2048,4096]{1,0:T(8,128)(2,1)} async-done(((bf16[256,4096]{1,0:T(8,128)(2,1)}), bf16[2048,4096]{1,0:T(8,128)(2,1)}) %all-gather.22.cloned.1.call-update) | async-done | bytes 16777232 | tf_op jit(solution)/shard_map/all_gather | solution.py:203
  453.5 35.9 fusion.137
  520.3 194.8 %while.114 = (s32[]{:T(128)}, f32[16,4096]{1,0:T(8,128)S(1)}, f32[16,16,4096]{2,1,0:T(8,128)}, f32[16,32,4096]{2,1,0:T(8,128)}, f32[16,4096]{1,0:T(8,128)S(1)}, ...) while((s32[]{:T(128)}, f32[16,4096]{1,0:T(8,128)S(1)}, ...), condition=%wide.region_3.4_spmd.clone, body=%wide.region_2.3_spmd.clone.sunk | while | flops 8519714 | bytes 4463724 | solution.py:82
  716.5 21.2 all-gather.28.cloned.1.call-done
  754.5 273.4 %while.113 = (s32[]{:T(128)}, f32[16,4096]{1,0:T(8,128)S(1)}, f32[16,32,4096]{2,1,0:T(8,128)}, f32[16,16,4096]{2,1,0:T(8,128)}, f32[16,32,4096]{2,1,0:T(8,128)},...) while((s32[]{:T(128)}, f32[16,4096]{1,0:T(8,128)S(1)}, ...), condition=%wide.region_39.40_spmd, body=%wide.region_6.39_spmd.sunk | while | flops 18743328 | bytes 13908669 | solution.py:82
  1036.4 450.3 %while.116 = (s32[]{:T(128)}, f32[16,4096]{1,0:T(8,128)S(1)}, f32[16,4096]{1,0:T(8,128)S(1)}, f32[16,32,4096]{2,1,0:T(8,128)}, f32[16,32,4096]{2,1,0:T(8,128)}, ...) while((s32[]{:T(128)}, f32[16,4096]{1,0:T(8,128)S(1)}, ...), condition=%wide.region_169.170_spmd.clone, body=%wide.region_40.169_spmd.clone.sunk | while | flops 75659264 | bytes 42547676 | solution.py:82
  1548.2 875.3 %while.118 = (s32[]{:T(128)}, f32[16,4096]{1,0:T(8,128)S(1)}, f32[16,4096]{1,0:T(8,128)S(1)}, f32[16,32,4096]{2,1,0:T(8,128)}, f32[16,32,4096]{2,1,0:T(8,128)}, ...) while((s32[]{:T(128)}, f32[16,4096]{1,0:T(8,128)S(1)}, ...), condition=%wide.region_269.270_spmd.clone, body=%wide.region_172.269_spmd.clone.sunk | while | flops 168639488 | bytes 69718392 | solution.py:82
  2436.8 15.7 fusion.210
  2460.8 47.6 %fusion.207 = (f32[4096]{0:T(1024)}, f32[4096]{0:T(1024)}, f32[4096]{0:T(1024)}, f32[4096]{0:T(1024)}, f32[4096]{0:T(1024)}, /*index=5*/bf16[512,4096]{1,0:T(8,1...) fusion(f32[512,8192]{1,0:T(8,128)} %fusion.224, ...), kind=kOutput, calls=%fused_computation.1128 | convolution fusion | flops 763834368 | bytes 123322368 | tf_op jit(solution)/shard_map/dot_general | solution.py:241
  2514.1 17.5 fusion.160
  2547.7 29.3 fusion.148
  2577.0 65.0 %pad_maximum_fusion = f32[2048,12288]{1,0:T(8,128)} fusion(f32[2048,4096]{1,0:T(8,128)} %fusion.160, f32[2048,8192]{1,0:T(8,128)} %fusion.148), kind=kLoop, calls=%fused_computation.991 | loop fusion | flops 25165824 | bytes 201326592 | tf_op jit(solution)/shard_map/concatenate | solution.py:297
  2648.8 820.3 %reduce-scatter.8.cloned.1.call-done = f32[64,12288]{1,0:T(8,128)} async-done(((f32[2048,12288]{1,0:T(8,128)}), f32[64,12288]{1,0:T(8,128)}) %reduce-scatter.8.cloned.1.call-update) | async-done | bytes 3145744 | tf_op jit(solution)/shard_map/reduce_scatter | solution.py:296
  3474.3 15.0 fusion.159
  3489.3 25.6 fusion.156
  3521.2 28.9 all-reduce.243
  3552.9 16.0 all-reduce.234
  3587.2 69.2 %all-gather.24.cloned.1.call-done = bf16[256,12288]{1,0:T(8,128)(2,1)} async-done(((bf16[64,12288]{1,0:T(8,128)(2,1)}), bf16[256,12288]{1,0:T(8,128)(2,1)}) %all-gather.24.cloned.1.call-update) | async-done | bytes 6291472 | tf_op jit(solution)/shard_map/all_gather | solution.py:302
  3665.0 49.1 %all-reduce.240.cloned.1.call-done = f32[1,16,4096]{2,1,0:T(8,128)} async-done(((f32[1,16,4096]{2,1,0:T(8,128)}), f32[1,16,4096]{2,1,0:T(8,128)}) %all-reduce.240.cloned.1.call-update) | async-done | bytes 262160 | tf_op jit(solution)/shard_map/psum | solution.py:281
  (2251 shorter events, 2049.4 us)
Async XLA Ops:
  7.2 294.0 %all-gather.16.cloned.1.call-start = ((), (), s32[]{:S(2)}) async-start(), calls=%async_computation.5 | async-start | bytes 37748736 | tf_op jit(solution)/shard_map/all_gather | solution.py:143
  7.9 445.5 %all-gather.22.cloned.1.call-start = ((), (), s32[]{:S(2)}) async-start(), calls=%async_computation.8 | async-start | bytes 18874368 | tf_op jit(solution)/shard_map/all_gather | solution.py:203
  8.7 480.7 %all-gather.18.cloned.1.call-start = ((), (), s32[]{:S(2)}) async-start(), calls=%async_computation.6 | async-start | bytes 1474560 | tf_op jit(solution)/shard_map/all_gather | solution.py:156
  9.4 490.7 %all-gather.20.cloned.1.call-start = ((), (), s32[]{:S(2)}) async-start(), calls=%async_computation.7 | async-start | bytes 1179648 | tf_op jit(solution)/shard_map/all_gather | solution.py:157
  10.0 706.5 %all-gather.26.cloned.1.call-start = ((), (), s32[]{:S(2)}) async-start(), calls=%async_computation.15 | async-start | bytes 1179648 | tf_op jit(solution)/shard_map/all_gather | solution.py:23
  54.2 399.2 %copy-start.40 = (f32[1,4096]{1,0:T(1,128)}, f32[1,4096]{1,0:T(1,128)S(1)}, u32[]{:S(2)}) copy-start(f32[1,4096]{1,0:T(1,128)S(1)} %get-tuple-element.2109) | copy-start | bytes 49156
  54.2 399.2 %copy-start.42 = (f32[1,4096]{1,0:T(1,128)}, f32[1,4096]{1,0:T(1,128)S(1)}, u32[]{:S(2)}) copy-start(f32[1,4096]{1,0:T(1,128)S(1)} %get-tuple-element.2110) | copy-start | bytes 49156
  54.3 399.2 %copy-start.44 = (f32[1,4096]{1,0:T(1,128)}, f32[1,4096]{1,0:T(1,128)S(1)}, u32[]{:S(2)}) copy-start(f32[1,4096]{1,0:T(1,128)S(1)} %get-tuple-element.2111) | copy-start | bytes 49156
  329.4 62.2 %collective-permute-start = (bf16[3,4096]{1,0:T(4,128)(2,1)S(1)}, bf16[3,4096]{1,0:T(4,128)(2,1)S(1)}, u32[]{:S(2)}, u32[]{:S(2)}) collective-permute-start(bf16[3,4096]{1,0:T(4,128)(2,1)S(1)} %slice.3467), channel_id=1, source_target_pairs={{0,1},{1,2},{2,3},{3,4},{4,5},{5,6},{6,7},{8,9},{9,10},{10,11},{11... | collective-permute-start | bytes 73736 | tf_op jit(solution)/shard_map/ppermute | solution.py:17
  517.7 220.0 %all-gather.28.cloned.1.call-start = ((), (), s32[]{:S(2)}) async-start(), calls=%async_computation.16 | async-start | bytes 1179648 | tf_op jit(solution)/shard_map/all_gather | solution.py:23
  715.8 813.5 %all-gather.30.cloned.1.call-start = ((), (), s32[]{:S(2)}) async-start(), calls=%async_computation.17 | async-start | bytes 1179648 | tf_op jit(solution)/shard_map/all_gather | solution.py:42
  1036.3 454.1 %copy-start.56 = (bf16[512]{0:T(512)(128)(2,1)S(1)}, bf16[512]{0:T(512)(128)(2,1)}, u32[]{:S(2)}) copy-start(bf16[512]{0:T(512)(128)(2,1)} %param.40) | copy-start | bytes 3076
  1487.5 1157.9 %reduce-scatter.12.cloned.1.call-start = ((), (), s32[]{:S(2)}) async-start(), calls=%async_computation.13 | async-start | bytes 2359296 | tf_op jit(solution)/shard_map/reduce_scatter | solution.py:276
  1548.2 875.3 %copy-start.20 = (f32[16,32,16]{2,1,0:T(8,128)S(1)}, f32[16,32,16]{2,1,0:T(8,128)}, u32[]{:S(2)}) copy-start(f32[16,32,16]{2,1,0:T(8,128)} %copy-done.19) | copy-start | bytes 98308
  2456.9 190.1 %reduce-scatter.10.cloned.1.call-start = ((), (), s32[]{:S(2)}) async-start(), calls=%async_computation.12 | async-start | bytes 2949120 | tf_op jit(solution)/shard_map/reduce_scatter | solution.py:275
  2510.2 34.4 collective-permute-start.1
  2514.1 955.1 %reduce-scatter.8.cloned.1.call-start = ((), (), s32[]{:S(2)}) async-start(), calls=%async_computation.10 | async-start | bytes 103809024 | tf_op jit(solution)/shard_map/reduce_scatter | solution.py:296
  2642.0 830.4 %copy-start.57 = (u32[32]{0:T(128)S(1)}, u32[32]{0:T(128)}, u32[]{:S(2)}) copy-start(u32[32]{0:T(128)} %constant.751) | copy-start | bytes 388
  2642.0 832.3 %copy-start.4 = (bf16[1,512,2048]{2,1,0:T(8,128)(2,1)S(1)}, bf16[1,512,2048]{2,1,0:T(8,128)(2,1)}, u32[]{:S(2)}) copy-start(bf16[1,512,2048]{2,1,0:T(8,128)(2,1)} %param.28) | copy-start | bytes 6291460
  2642.1 909.0 %reduce-scatter.16.cloned.1.call-start = ((), (), s32[]{:S(2)}) async-start(), calls=%async_computation.18 | async-start | bytes 2359296
  2644.8 907.4 %reduce-scatter.14.cloned.1.call-start = ((), (), s32[]{:S(2)}) async-start(), calls=%async_computation.14 | async-start | bytes 294912 | tf_op jit(solution)/shard_map/reduce_scatter | solution.py:278
  2645.4 938.6 %all-reduce.242.cloned.1.call-start = ((), (), s32[]{:S(2)}) async-start(), calls=%async_computation.19 | async-start | bytes 589824 | tf_op jit(solution)/shard_map/psum | solution.py:311
  2648.8 1007.6 %all-gather.24.cloned.1.call-start = ((), (), s32[]{:S(2)}) async-start(), calls=%async_computation.11 | async-start | bytes 7864320 | tf_op jit(solution)/shard_map/all_gather | solution.py:302
  3472.3 241.8 %all-reduce.240.cloned.1.call-start = ((), (), s32[]{:S(2)}) async-start(), calls=%async_computation.9 | async-start | bytes 524288 | tf_op jit(solution)/shard_map/psum | solution.py:281
  (51 other events, 2901.6 us)
Sparse Core Ops, SparseCore 0:
  9.6 291.4 all-gather.15
  302.8 150.6 all-gather.21
  455.0 21.9 all-gather.17
  478.5 21.6 all-gather.19
  517.8 21.7 all-gather.25
  715.9 21.6 all-gather.27
  1487.6 21.7 all-gather.29
  2457.1 34.1 reduce-scatter.11
  2514.2 38.0 reduce-scatter.9
  2642.2 826.9 reduce-scatter.7
  3471.4 34.8 reduce-scatter.15
  3509.0 29.5 reduce-scatter.13
  3542.4 41.4 all-reduce.241
  3586.2 70.1 all-gather.23
  3659.1 54.9 all-reduce.239
where the time goes:
time: 3740 us; the launch traced here: 3720 us
  other arithmetic  1470 us (39%)
  waiting for transfers between devices  1290 us (34%)
  local copies, waits for them, and re-layouts  548 us (15%)
  matrix products  226 us (6%)
  blocking collectives  151 us (4%)
    reduce_scatter x1, waiting for transfers between devices, shards(): lax.psum_scatter(jnp.concatenate([in_part, out_part], axis=1), ('doc', 's...  820 us
    reduce_sum x608, other arithmetic, scan_block(): blk_rows[2][position][:, None] * blk_rows[1][position][None, :]  552 us
    reduce_sum x256, other arithmetic, scan_block(): decay_now = jnp.exp(blk_rows[0][position][None, :] * neg_rate)  277 us
    all_gather x1, waiting for transfers between devices, shards(): rows_in = lax.all_gather(in_weight, 'seq', axis=0, tiled=True)  245 us
    reduce_sum x272, other arithmetic, scan_block(): outputs.append(jnp.sum(blk_rows[3][position][:, None] * state_now, axis=0))  203 us
    slice x128, local copies, waits for them, and re-layouts, scan_block(): decay_now = jnp.exp(blk_rows[0][position][None, :] * neg_rate)  165 us
    slice x128, local copies, waits for them, and re-layouts, scan_block(): blk_rows[1][position][None, :]  159 us
    dynamic_update_slice x128, other arithmetic, run_blocks(): lax.scan(jax.checkpoint(block_step), state_now, blocked)  127 us
  transfers between devices with their start and end apart: 17, of which 8 were waited for; matrix products, arithmetic and copies ran while one was open for 15% of the time, Pallas kernels for 0%

commit v1 on v0

v1 whole, which is shorter than its diff:
```python
import functools
import jax
import jax.numpy as jnp
from jax import lax
from jax.experimental import pallas as pl
from jax.experimental.pallas import tpu as pltpu
from jax.sharding import PartitionSpec as P

TB = 16
F32 = jnp.float32
BF = jnp.bfloat16
LN2 = 0.6931471805599453
NORM_EPS = 1e-05
LAST = (((1,), (1,)), ((), ()))
FIRST = (((0,), (0,)), ((), ()))


def mm(a, b):
    return jnp.dot(a, b, preferred_element_type=F32)


def mm_last(a, b):
    return lax.dot_general(a, b, LAST, preferred_element_type=F32)


def mm_first(a, b):
    return lax.dot_general(a, b, FIRST, preferred_element_type=F32)


def cost(us):
    return pl.CostEstimate(flops=int(us * 1.0e9), bytes_accessed=0, transcendentals=0)


def params():
    return pltpu.CompilerParams(vmem_limit_bytes=56 * 2**20)


def shape(dims, kind=F32):
    return jax.ShapeDtypeStruct(dims, kind)


def whole(dims):
    return pl.BlockSpec(dims, lambda *_: (0,) * len(dims))


def tie(x, *tokens):
    free = pl.BlockSpec(memory_space=pl.ANY)
    return pl.pallas_call(lambda *refs: None, out_shape=shape(x.shape, x.dtype),
                          in_specs=[free] * (1 + len(tokens)), out_specs=free, input_output_aliases={0: 0},
                          name="tie")(x, *tokens)


def sigmoid(x):
    return 0.5 + 0.5 * jnp.tanh(0.5 * x)


def tiles(x):
    return sum(x[:, c:c + 128] for c in range(0, x.shape[1], 128))


def softplus(x):
    return jnp.maximum(x, 0.0) + jnp.log1p(jnp.exp(-jnp.abs(x)))


def front_kernel(first_ref, top_ref, low_ref, halo_ref, w_ref, few_ref, xproj_ref, init_ref, *refs, lead):
    taps, shift = few_ref[:lead + 1].astype(F32), few_ref[lead + 1:lead + 2].astype(F32)
    normed_ref, inner_ref, mixed_ref, rim_ref, proj_ref, xs_ref = refs[-6:]
    step, width = top_ref.shape[0], xs_ref.shape[1]

    def normalise(x):
        r = x.astype(F32)
        scale = lax.rsqrt(jnp.mean(r * r, axis=1, keepdims=True) + NORM_EPS)
        return (r * scale).astype(BF)

    @pl.when(pl.program_id(0) == 0)
    def _():
        before = mm(normalise(halo_ref[...]), w_ref[...])[halo_ref.shape[0] - 8:]
        rim = jnp.where(first_ref[0] == 1, init_ref[...], before)
        rim_ref[0] = rim
        xs_ref[:8] = rim

    in_top = 2 * pl.program_id(0) < pl.num_programs(0)
    normed_ref[...] = normalise(jnp.where(in_top, top_ref[...], low_ref[...]))
    x = mm(normed_ref[...], w_ref[...])
    inner_ref[0] = x
    xs_ref[8:] = x
    for c in range(0, width, 256):
        cs = pl.ds(c, 256)
        pre = shift[:, c:c + 256]
        for tap in range(lead + 1):
            pre = pre + taps[tap:tap + 1, c:c + 256] * xs_ref[pl.ds(8 - lead + tap, step), cs]
        mixed_ref[0, :, cs] = (pre * sigmoid(pre)).astype(BF)
    proj_ref[...] = mm_last(mixed_ref[0], xproj_ref[...])
    xs_ref[:8] = xs_ref[step:step + 8]


def front(slot, docs, kept, first, top, low, halo, w, small, lead, cols, init, step=128):
    width, block = w.shape
    extra = 16
    tokens = 2 * top.shape[0]
    count = tokens // step
    rows = pl.BlockSpec((1, step, block), lambda k: (slot, k, 0))
    few = pl.BlockSpec((1, 8, block), lambda k: (slot, 0, 0))
    return pl.pallas_call(
        functools.partial(front_kernel, lead=lead),
        out_shape=[shape((docs * tokens, width), BF), shape((docs, tokens, block)), shape((docs, tokens, block), BF),
                   shape((docs, 8, block)), shape((tokens, cols))],
        grid=(count,),
        in_specs=[pl.BlockSpec(memory_space=pltpu.SMEM), pl.BlockSpec((step, width), lambda k: (jnp.minimum(k, count // 2 - 1), 0)),
                  pl.BlockSpec((step, width), lambda k: (jnp.maximum(k - count // 2, 0), 0)),
                  pl.BlockSpec((extra, width), lambda k: (0, 0)), whole(w.shape),
                  whole((16, block)), pl.BlockSpec((cols, block), lambda k: (1, 0)), whole((8, block))]
        + [pl.BlockSpec(memory_space=pl.ANY)] * len(kept),
        out_specs=[pl.BlockSpec((step, width), lambda k: (slot * count + k, 0)), rows, rows, few,
                   pl.BlockSpec((step, cols), lambda k: (k, 0))],
        scratch_shapes=[pltpu.VMEM((step + 8, block), F32)],
        input_output_aliases={8 + i: i for i in range(len(kept))},
        compiler_params=params(), cost_estimate=cost(0.1), name="front",
    )(first, top, low, halo, w, small, small, init, *kept)


def summary_kernel(rank_ref, dtw_ref, shift_ref, mixed_ref, bt_ref, rate_ref, *refs):
    pre_ref, delta_ref, end_ref, decay_ref = refs[-4:]
    tokens, width = mixed_ref.shape[1:]
    rate = rate_ref[...]
    count = tokens // TB

    def steps(i):
        rows = pl.ds(pl.multiple_of(i * TB, TB), TB)
        pre = mm(rank_ref[0, rows], dtw_ref[...]) + shift_ref[...]
        pre_ref[0, rows] = pre
        delta_ref[0, rows] = softplus(pre)

    steps(0)

    def body(i, carry):
        h, total = carry
        rows = pl.ds(pl.multiple_of(i * TB, TB), TB)
        dl = delta_ref[0, rows]
        dr = dl * mixed_ref[0, rows].astype(F32)
        bt = bt_ref[0, i]
        for t in range(TB):
            h = jnp.exp2(dl[t:t + 1] * rate) * h + bt[:, t:t + 1] * dr[t:t + 1]
        steps(jnp.minimum(i + 1, count - 1))
        return h, total + dl

    h, total = lax.fori_loop(0, count, body, (jnp.zeros(rate.shape, F32), jnp.zeros((TB, width), F32)))
    end_ref[0] = h
    decay_ref[0] = jnp.exp2(jnp.sum(total, axis=0, keepdims=True) * rate)


def chained(kept, before):
    return [pl.BlockSpec(memory_space=pl.ANY)] * len(kept), {before + i: i for i in range(len(kept))}


def summary(base, count, kept, rank_in, dtw, shift, mixed, bt, rate):
    docs, tokens, width = mixed.shape
    n, rank = rate.shape[0], rank_in.shape[2]
    rows = pl.BlockSpec((1, tokens, width), lambda g: (g + base, 0, 0))
    state = pl.BlockSpec((1, n, width), lambda g: (g, 0, 0))
    free, alias = chained(kept, 6)
    return pl.pallas_call(
        summary_kernel,
        out_shape=[shape((docs, tokens, width))] * 2 + [shape((count, n, width))] * 2,
        grid=(count,),
        in_specs=[pl.BlockSpec((1, tokens, rank), lambda g: (g + base, 0, 0)), whole(dtw.shape), whole((1, width)), rows,
                  pl.BlockSpec((1, tokens // TB, n, TB), lambda g: (g + base, 0, 0, 0)), whole(rate.shape)] + free,
        out_specs=[rows, rows, state, state], input_output_aliases=alias,
        compiler_params=params(), cost_estimate=cost(22), name="summary",
    )(rank_in, dtw, shift, mixed, bt, rate, *kept)


def forward_kernel(delta_ref, mixed_ref, gate_ref, dg_ref, bt_ref, cdiag_ref, rate_ref, start_ref, mask_ref, skip_ref,
                   *refs):
    dy_ref, before_ref, gated_ref, dgate_ref, dout_ref, dstart_ref, sgrad_ref, hs_ref, ps_ref, hb_ref, zb_ref, sb_ref = refs[-12:]
    tokens = delta_ref.shape[1]
    n = rate_ref.shape[0]
    count = tokens // TB
    rate = rate_ref[...]

    @pl.when(pl.program_id(1) == 0)
    def _():
        hs_ref[...] = start_ref[0]
        ps_ref[...] = jnp.ones_like(ps_ref)
        dstart_ref[0] = jnp.zeros(dstart_ref.shape[1:], F32)
        sgrad_ref[0] = jnp.zeros(sgrad_ref.shape[1:], F32)

    mask = mask_ref[...]
    spread = lax.rem(lax.broadcasted_iota(jnp.int32, mask.shape, 1), n) == lax.broadcasted_iota(jnp.int32, mask.shape, 0)

    def finish(i, hm, good):
        rows = pl.ds(pl.multiple_of(i * TB, TB), TB)
        gate, dg = gate_ref[0, rows], dg_ref[0, rows]
        sig = sigmoid(gate)
        act = gate * sig
        mx = mixed_ref[0, rows].astype(F32)
        dy = dg * act
        dy_ref[0, rows] = dy
        sgrad_ref[0] += jnp.where(good, dy * mx, 0.0)
        y = mm(cdiag_ref[0, i], hm) + skip_ref[...] * mx
        gated_ref[0, rows] = (y * act).astype(BF)
        dgate_ref[0, rows] = (dg * y * (sig * (1.0 + gate * (1.0 - sig)))).astype(BF)
        dout_ref[0, i] = mm_last(jnp.ones((8, 128), BF), sb_ref[...])[:1]
        weight = jnp.where(spread, jnp.sum(cdiag_ref[0, i].astype(F32), axis=0, keepdims=True), 0.0).astype(BF)
        dstart_ref[0] += jnp.where(good, mm(weight, zb_ref[...]), 0.0)

    def body(i, carry):
        h, p = carry
        rows = pl.ds(pl.multiple_of(i * TB, TB), TB)
        dl = delta_ref[0, rows]
        dr = dl * mixed_ref[0, rows].astype(F32)
        gate = gate_ref[0, rows]
        dy = dg_ref[0, rows] * gate * sigmoid(gate)
        bt = bt_ref[0, i]
        hb = h.astype(BF)
        before_ref[0, pl.ds(pl.multiple_of(i * TB * n, TB * n), n)] = hb
        last = jnp.maximum(i - 1, 0)
        finish(last, before_ref[0, pl.ds(pl.multiple_of((last * TB + 1) * n, n), TB * n)], i > 0)
        for t in range(TB):
            if t:
                before_ref[0, pl.ds(pl.multiple_of((i * TB + t) * n, n), n)] = hb
            a = jnp.exp2(dl[t:t + 1] * rate)
            h = a * h + bt[:, t:t + 1] * dr[t:t + 1]
            hb = h.astype(BF)
            sb_ref[t * n:(t + 1) * n] = tiles(h * dy[t:t + 1]).astype(BF)
            p = p * a
            zb_ref[t * n:(t + 1) * n] = (p * dy[t:t + 1]).astype(BF)
        return h, p

    h, p = lax.fori_loop(0, count, body, (hs_ref[...], ps_ref[...]))
    hs_ref[...] = h
    ps_ref[...] = p
    hb_ref[:(TB - 1) * n] = before_ref[0, ((count - 1) * TB + 1) * n:count * TB * n]
    hb_ref[(TB - 1) * n:] = h.astype(BF)
    finish(count - 1, hb_ref[...], True)


def forward(base, part, kept, delta, mixed, gate, d_gated, bt, cdiag, rate, start, mask, skip, step=128):
    docs, tokens, width = delta.shape
    n, nb = rate.shape[0], step // TB
    rows = pl.BlockSpec((1, step, width), lambda g, k: (g + base, k, 0))
    own = pl.BlockSpec((1, step, width), lambda g, k: (g, k, 0))
    state = pl.BlockSpec((1, n, width), lambda g, k: (g, 0, 0))
    cols = pl.BlockSpec((1, nb, n, TB), lambda g, k: (g + base, k, 0, 0))
    free, alias = chained(kept, 10)
    return pl.pallas_call(
        forward_kernel,
        out_shape=[shape(delta.shape), shape((docs, tokens * n, width), BF), shape(delta.shape, BF), shape(delta.shape, BF),
                   shape((docs, tokens // TB, 1, TB * n)), shape((part, n, width)), shape((part, TB, width))],
        grid=(part, tokens // step),
        in_specs=[rows, rows, rows, own, cols, pl.BlockSpec((1, nb, TB, TB * n), lambda g, k: (g + base, k, 0, 0)),
                  whole(rate.shape), state, whole(mask.shape), whole((1, width))] + free,
        out_specs=[rows, pl.BlockSpec((1, step * n, width), lambda g, k: (g + base, k, 0)), rows, rows,
                   pl.BlockSpec((1, nb, 1, TB * n), lambda g, k: (g + base, k, 0, 0)), state,
                   pl.BlockSpec((1, TB, width), lambda g, k: (g, 0, 0))],
        scratch_shapes=[pltpu.VMEM((n, width), F32), pltpu.VMEM((n, width), F32), pltpu.VMEM((TB * n, width), BF),
                        pltpu.VMEM((TB * n, width), BF), pltpu.VMEM((TB * n, 128), BF)],
        input_output_aliases=alias, compiler_params=params(), cost_estimate=cost(45), name="forward",
    )(delta, mixed, gate, d_gated, bt, cdiag, rate, start, mask, skip, *kept)


def backward_kernel(pre_ref, delta_ref, mixed_ref, dy_ref, before_ref, ct_ref, bdiag_ref, rate_ref, qin_ref, mask_ref, skip_ref,
                    *refs):
    dpre_ref, dmix_ref, din_ref, drate_ref, bgrad_ref, qout_ref, ps_ref, qb_ref, wb_ref, sb_ref = refs[-10:]
    tokens = delta_ref.shape[1]
    n = rate_ref.shape[0]
    count = tokens // TB
    rate = rate_ref[...]

    @pl.when(pl.program_id(1) == 0)
    def _():
        ps_ref[...] = qin_ref[0]
        drate_ref[0] = jnp.zeros(drate_ref.shape[1:], F32)
        bgrad_ref[0] = jnp.zeros(bgrad_ref.shape[1:], F32)

    mask = mask_ref[...]
    spread = lax.rem(lax.broadcasted_iota(jnp.int32, mask.shape, 1), n) == lax.broadcasted_iota(jnp.int32, mask.shape, 0)
    sums = jnp.concatenate([mask, spread.astype(F32)], axis=0).astype(BF)

    fold = jnp.ones((8, 128), BF)

    def finish(i, good, side):
        rows = pl.ds(pl.multiple_of(i * TB, TB), TB)
        dl = delta_ref[0, rows]
        mx = mixed_ref[0, rows].astype(F32)
        d_drive = mm(bdiag_ref[0, i], qb_ref[side])
        both = LN2 * mm(sums, wb_ref[side])
        din_ref[0, i] = mm_last(fold, sb_ref[side])[:1]
        drate_ref[0] += jnp.where(good, both[TB:], 0.0)
        sig = sigmoid(pre_ref[0, rows])
        d_pre = both[:TB] * jnp.where(dl > 1e-30, sig / dl, 1.0) + mx * d_drive * sig
        dpre_ref[0, rows] = d_pre.astype(BF)
        bgrad_ref[0] += jnp.where(good, d_pre, 0.0)
        dmix_ref[0, rows] = dl * d_drive + dy_ref[0, rows] * skip_ref[...]

    def scan(i, p, side):
        rows = pl.ds(pl.multiple_of(i * TB, TB), TB)
        dl = delta_ref[0, rows]
        dr = dl * mixed_ref[0, rows].astype(F32)
        dy = dy_ref[0, rows]
        ct = ct_ref[0, i]
        for t in reversed(range(TB)):
            q = ct[:, t:t + 1] * dy[t:t + 1] + p
            qb_ref[side, t * n:(t + 1) * n] = q.astype(BF)
            sb_ref[side, t * n:(t + 1) * n] = tiles(q * dr[t:t + 1]).astype(BF)
            x = dl[t:t + 1] * rate
            p = jnp.exp2(x) * q
            e = p * before_ref[0, pl.ds(pl.multiple_of((i * TB + t) * n, n), n)].astype(F32)
            wb_ref[side, t * n:(t + 1) * n] = (x * e).astype(BF)
        return p

    def body(j, p):
        i = count - 1 - 2 * j
        finish(jnp.minimum(i + 1, count - 1), j > 0, 1)
        p = scan(i, p, 0)
        finish(i, True, 0)
        return scan(i - 1, p, 1)

    ps_ref[...] = lax.fori_loop(0, count // 2, body, ps_ref[...])
    finish(0, True, 1)
    qout_ref[0] = ps_ref[...]


def backward(base, part, begin, kept, pre, delta, mixed, dy, before, ct, bdiag, rate, qin, mask, skip, step=128):
    docs, tokens, width = delta.shape
    n, nb, last = rate.shape[0], step // TB, (begin + tokens // 2) // step - 1
    rows = pl.BlockSpec((1, step, width), lambda g, k: (g + base, last - k, 0))
    state = pl.BlockSpec((1, n, width), lambda g, k: (g, 0, 0))
    line = pl.BlockSpec((1, nb, 1, TB * n), lambda g, k: (g + base, last - k, 0, 0))
    free, alias = chained(kept, 11)
    return pl.pallas_call(
        backward_kernel,
        out_shape=[shape(delta.shape, BF), shape(delta.shape), shape((docs, tokens // TB, 1, TB * n)),
                   shape((part, n, width)), shape((part, TB, width)), shape((part, n, width))],
        grid=(part, tokens // 2 // step),
        in_specs=[rows, rows, rows, rows, pl.BlockSpec((1, step * n, width), lambda g, k: (g + base, last - k, 0)),
                  pl.BlockSpec((1, nb, n, TB), lambda g, k: (g + base, last - k, 0, 0)),
                  pl.BlockSpec((1, nb, TB, TB * n), lambda g, k: (g + base, last - k, 0, 0)),
                  whole(rate.shape), state, whole(mask.shape), whole((1, width))] + free,
        out_specs=[rows, rows, line, state, pl.BlockSpec((1, TB, width), lambda g, k: (g, 0, 0)), state],
        scratch_shapes=[pltpu.VMEM((n, width), F32), pltpu.VMEM((2, TB * n, width), BF), pltpu.VMEM((2, TB * n, width), BF),
                        pltpu.VMEM((2, TB * n, 128), BF)],
        input_output_aliases=alias, compiler_params=params(), cost_estimate=cost(4), name="backward",
    )(pre, delta, mixed, dy, before, ct, bdiag, rate, qin, mask, skip, *kept)


def conv_back_kernel(dproj_ref, xproj_ref, dmix_ref, inner_ref, prev_ref, rim_ref, taps_ref, shift_ref, carry_ref, *refs,
                     lead, first):
    dinner_ref, tail_ref, head_ref, sums_ref, dm_ref, xs_ref, ds_ref = refs[-7:]
    step, width = dmix_ref.shape[1:]
    k = pl.program_id(1)

    @pl.when(k == 0)
    def _():
        ds_ref[step:] = carry_ref[0]
        sums_ref[0] = jnp.zeros(sums_ref.shape[1:], F32)

    dm_ref[...] = mm(dproj_ref[0], xproj_ref[...])
    xs_ref[:8] = jnp.where(k == pl.num_programs(1) - 1, rim_ref[0], prev_ref[0]) if first else prev_ref[0]
    xs_ref[8:] = inner_ref[0]
    cw = 256

    def tile(x):
        return jnp.sum(x.reshape(step // 8, 8, cw), axis=0)

    for c in range(0, width, cw):
        cs = pl.ds(c, cw)
        pre = shift_ref[:, cs]
        for tap in range(lead + 1):
            pre = pre + taps_ref[tap:tap + 1, cs] * xs_ref[pl.ds(8 - lead + tap, step), cs]
        sig = sigmoid(pre)
        d_conv = (dmix_ref[0, :, cs] + dm_ref[:, cs]) * (sig * (1.0 + pre * (1.0 - sig)))
        ds_ref[:step, cs] = d_conv
        sums_ref[0, :8, cs] += tile(d_conv)
        for tap in range(lead + 1):
            sums_ref[0, 8 + 8 * tap:16 + 8 * tap, cs] += tile(d_conv * xs_ref[pl.ds(8 - lead + tap, step), cs])
        back = taps_ref[lead:lead + 1, cs] * d_conv
        for m in range(1, lead + 1):
            back = back + taps_ref[lead - m:lead - m + 1, cs] * ds_ref[pl.ds(m, step), cs]
        dinner_ref[0, :, cs] = back.astype(BF)

        @pl.when(k == 0)
        def _():
            tail_ref[0, :, cs] = back[step - 8:]

        head_ref[0, :, cs] = d_conv[:8]
        ds_ref[step:, cs] = d_conv[:8]


def conv_back(begin, kept, carry, d_proj, xproj_t, d_mix, inner_x, rim, taps, shift, step=128):
    docs, tokens, width = d_mix.shape
    half = tokens // 2
    last = (begin + half) // step - 1
    count = half // step
    lead = taps.shape[0] - 1
    cols = xproj_t.shape[0]
    rows = pl.BlockSpec((1, step, width), lambda g, k: (g, last - k, 0))
    few = pl.BlockSpec((1, 8, width), lambda g, k: (g, 0, 0))
    sums = 8 * (lead + 2)
    free, alias = chained(kept, 9)
    return pl.pallas_call(
        functools.partial(conv_back_kernel, lead=lead, first=begin == 0),
        out_shape=[shape(d_mix.shape, BF), shape((docs, 8, width)), shape((docs, 8, width)), shape((docs, sums, width))],
        grid=(docs, count),
        in_specs=[pl.BlockSpec((1, step, cols), lambda g, k: (g, count - 1 - k, 0)), whole(xproj_t.shape), rows, rows,
                  pl.BlockSpec((1, 8, width), lambda g, k: (g, jnp.maximum((last - k) * (step // 8) - 1, 0), 0)), few,
                  whole(taps.shape), whole((1, width)), few] + free,
        out_specs=[rows, few, few, pl.BlockSpec((1, sums, width), lambda g, k: (g, 0, 0))],
        scratch_shapes=[pltpu.VMEM((step, width), F32), pltpu.VMEM((step + 8, width), F32), pltpu.VMEM((step + 8, width), F32)],
        input_output_aliases=alias, compiler_params=params(), cost_estimate=cost(0.2), name="conv_back",
    )(d_proj, xproj_t, d_mix, inner_x, inner_x, rim, taps, shift, carry, *kept)


def place_kernel(doc_ref, *refs, pieces):
    parts, (weight_ref, gain_ref, sum_ref) = refs[:pieces], refs[pieces:pieces + 3]
    out_ref, total_ref = refs[-2:]
    j = pl.program_id(0)

    def put(x):
        x = x.astype(F32)
        out_ref[...] = x * gain_ref[...]
        x = x * weight_ref[...].astype(F32)
        x = sum(x[:, c:c + 128] for c in range(0, x.shape[1], 128))
        total_ref[...] = jnp.where(j == 0, sum_ref[...], total_ref[...]) + x

    if pieces == 1:
        put(parts[0][...])
    else:
        for p in range(pieces):
            @pl.when(j == p)
            def _():
                put(parts[p][...])


def place(doc, kept, parts, weight, gain, sums, block, offset):
    rows, width = weight.shape
    docs = width // 2 // block
    at = (lambda j, doc_ref: (0, offset + j)) if len(parts) == 1 else (lambda j, doc_ref: (0, offset + (doc_ref[0] ^ j)))
    one = lambda j, doc_ref: (0, 0)
    piece_at = (lambda j, doc_ref: (0, j)) if len(parts) == 1 else one
    free = [pl.BlockSpec(memory_space=pl.ANY)] * len(kept)
    return pl.pallas_call(
        functools.partial(place_kernel, pieces=len(parts)),
        out_shape=[shape((rows, width)), shape((rows, 128))],
        grid_spec=pltpu.PrefetchScalarGridSpec(
            num_scalar_prefetch=1, grid=(docs,),
            in_specs=[pl.BlockSpec((rows, block), piece_at)] * len(parts)
            + [pl.BlockSpec((rows, block), at), pl.BlockSpec((rows, 1), one), pl.BlockSpec((rows, 128), one)] + free,
            out_specs=[pl.BlockSpec((rows, block), at), pl.BlockSpec((rows, 128), one)]),
        input_output_aliases={4 + len(parts): 0} if kept else {},
        compiler_params=params(), cost_estimate=cost(0.1), name="place",
    )(doc, *parts, weight, gain, sums, *kept)


def input_kernel(part_ref, one_ref, two_ref, hidden_ref, cot_ref, out_ref):
    d_normed = part_ref[...] + one_ref[...].astype(F32) + two_ref[...].astype(F32)
    r = hidden_ref[...].astype(F32)
    scale = lax.rsqrt(jnp.mean(r * r, axis=1, keepdims=True) + NORM_EPS)
    scaled = r * scale
    out_ref[...] = cot_ref[...].astype(F32) + scale * (d_normed - scaled * jnp.mean(d_normed * scaled, axis=1, keepdims=True))


def input_gradient(part, one, two, hidden, cot, step=128):
    rows = pl.BlockSpec((step, hidden.shape[1]), lambda k: (k, 0))
    return pl.pallas_call(
        input_kernel, out_shape=shape(hidden.shape), grid=(hidden.shape[0] // step,),
        in_specs=[rows] * 5, out_specs=rows, compiler_params=params(), cost_estimate=cost(0.1), name="input_gradient",
    )(part, one, two, hidden, cot)


def shifted(block, axis, distance):
    devices = range(lax.axis_size(axis))
    route = [(i - distance, i) for i in devices if i - distance in devices]
    return lax.ppermute(block, axis, route)


def swap(x, axis, flip):
    return lax.ppermute(x, axis, [(i, i ^ flip) for i in range(lax.axis_size(axis))])


def piece(x, index, size, axis):
    return lax.dynamic_slice_in_dim(x, index * size, size, axis)


def chain(decays, states, order, keep, start):
    state = start
    for k in order:
        decay = decays[k].astype(F32)
        state = jnp.where(keep(k), decay * state + states[k].astype(F32), state)
    return state


def doc_gather(x):
    return [x] + [swap(x, "doc", j) for j in (1, 2, 3)]


def doc_sum(parts):
    total = parts[0].astype(F32)
    for j in (1, 2, 3):
        total = total + swap(parts[j].astype(BF), "doc", j).astype(F32)
    return total


def doc_place(parts, doc, axis):
    stack = jnp.stack(parts)
    return jnp.concatenate([lax.dynamic_index_in_dim(stack, doc ^ k, 0, False) for k in range(len(parts))], axis=axis)


def shards(hidden_in, cotangent, scan_init, conv_init, norm_gain, in_weight, conv_weight, conv_bias,
           xproj_weight, dt_weight, dt_bias, a_log, skip_d, out_weight):
    docs, seqs = lax.axis_size("doc"), lax.axis_size("seq")
    doc, seq = lax.axis_index("doc"), lax.axis_index("seq")
    near = seqs == 2 * docs == 8
    hidden, cot = hidden_in[0], cotangent[0]
    tokens, width = hidden.shape
    inner = in_weight.shape[1] // 2
    rank = dt_weight.shape[0]
    states = a_log.shape[0]
    lead = conv_init.shape[1]
    taps = conv_weight.shape[0]
    block = inner // docs
    rows_all = docs * tokens
    blocks = tokens // TB
    middle = tokens // 2
    slots = range(docs)

    def mine(x, offset=0):
        return lax.dynamic_slice_in_dim(x, offset + doc * block, block, x.ndim - 1)

    def mine_of(x, owner):
        return piece(x, owner, block, 1)

    def seq_gather(x):
        return lax.all_gather(x, "seq", axis=0, tiled=True)

    state_rows, lead_rows = states * block // width, 2 * (-(-lead * block // (2 * width)))

    def first_of(j):
        rows = mine_of(conv_init[0], doc ^ j)
        rows = jnp.pad(rows, ((0, lead_rows * width // block - lead), (0, 0))).reshape(lead_rows, width)
        start = mine_of(scan_init[0], doc ^ j).astype(BF).reshape(state_rows, width)
        packed = jnp.concatenate([hidden[tokens - 16:], start, rows], axis=0)
        return jnp.pad(packed, ((0, 32 - packed.shape[0]), (0, 0)))

    halo = [lax.ppermute(first_of(j), ("doc", "seq"),
                         [(d * seqs + s, (d ^ j) * seqs + (s + 1) % seqs) for d in slots for s in range(seqs)])
            for j in slots]
    top, low = hidden[:middle], tie(hidden[middle:], *halo)
    one, two = ([swap(x, "doc", j) for x in (top, low)] for j in (1, 2))
    scaled_weight = (in_weight.astype(F32) * norm_gain.astype(F32)[:, None]).astype(BF)
    w_inner = seq_gather(mine(scaled_weight))
    few = jnp.concatenate([conv_weight, conv_bias[None], dt_bias[None], skip_d[None]], axis=0)
    few = jnp.pad(few, ((0, 16 - few.shape[0]), (0, 0)))
    small = jnp.concatenate([few, a_log, dt_weight, xproj_weight.T], axis=0)
    if near:
        route = [((d, 2 * z + c), (z, 2 * d + c)) for d in slots for z in slots for c in range(2)]
        turn = [(a * seqs + b, e * seqs + f) for (a, b), (e, f) in route]
        half = lax.ppermute(small, ("doc", "seq"), turn)
        half = tie(half, *one, *two)
        other = swap(half, "seq", 1)
        core = seq % 2 == 0
        small = jnp.concatenate([jnp.where(core, half, other), jnp.where(core, other, half)], axis=1)
    else:
        small = mine(lax.all_gather(small, "seq", axis=1, tiled=True))
    three = [swap(two[0], "doc", 1), swap(one[1], "doc", 2)]
    w_gate = seq_gather(tie(mine(scaled_weight, inner), small))
    w_out = seq_gather(mine(out_weight))

    wide = small.astype(F32)
    conv_taps, conv_shift, dt_shift, skip = wide[:taps], wide[taps][None], wide[taps + 1][None], wide[taps + 2][None]
    at = 16
    rate = -jnp.exp(wide[at:at + states])
    dt_full = small[at + states:at + states + rank]
    xproj_t = small[at + states + rank:]
    rate2 = rate * (1.0 / LN2)

    is_first = (seq == 0).astype(jnp.int32)[None]

    def first_rows(x):
        rows = x[16 + state_rows:16 + state_rows + lead_rows].reshape(-1, block)[:lead].astype(F32)
        return jnp.pad(rows, ((8 - lead, 0), (0, 0)))

    kept, proj_part = (), []
    for j, x in enumerate(((top, low), one, two, three)):
        if j == 3:
            x = [tie(half, kept[0]) for half in three]
            cot_top = tie(cot[:middle], *x)
            cot_near = [swap(cot_top, "doc", 1), swap(cot_top, "doc", 2)]
        *kept, part = front(j, docs, kept, is_first, *x, halo[j], w_inner, small, lead,
                            rank + 2 * states, first_rows(halo[j]))
        proj_part.append(part)
    normed, inner_x, mixed, rim = kept
    mixed_flat = mixed.reshape(rows_all, block)

    w_gate = tie(w_gate, *proj_part)
    gate_in = mm(normed, w_gate)
    got = [tie(swap(proj_part[j].astype(BF), "doc", j), gate_in) for j in slots[1:]]
    proj_own = (proj_part[0] + sum(x.astype(F32) for x in got)).astype(BF)
    proj = jnp.concatenate(doc_gather(proj_own), axis=0)
    proj = tie(proj, *cot_near)
    cot_low = tie(cot[middle:], proj)
    cot_rest = [swap(cot_low, "doc", 1), swap(cot_low, "doc", 2)]
    cot_far = [swap(tie(cot_near[1], proj), "doc", 1)]
    init = jnp.stack([x[16:16 + state_rows].reshape(states, block) for x in halo]).astype(F32)
    rank_in = proj[:, :rank]
    gate_in = gate_in.reshape(docs, tokens, block)

    mask = jnp.repeat(jnp.eye(TB, dtype=F32), states, axis=1)
    spread = jnp.tile(jnp.eye(states, dtype=BF), (1, TB))

    def columns(x):
        return jnp.swapaxes(x.reshape(docs, blocks, TB, states), 2, 3).astype(F32)

    def diagonal(x):
        return (mm(x, spread).reshape(docs, blocks, TB, TB * states) * mask).astype(BF)

    b_rows, c_rows = proj[:, rank:rank + states], proj[:, rank + states:]
    b_cols, c_cols = columns(b_rows), columns(c_rows)
    b_diag, c_diag = diagonal(b_rows), diagonal(c_rows)

    rank_in = rank_in.reshape(docs, tokens, rank)
    part = docs // 2
    starts, decays = {}, {}
    kept = ()
    for base in (part, 0):
        *kept, end_state, decay = summary(base, part, kept, rank_in, dt_full, dt_shift, mixed, b_cols, rate2)
        if base == 0:
            end_state = tie(end_state, *cot_far)
        ends = lax.all_gather(jnp.stack([end_state, decay]).astype(BF), "seq")
        decays[base] = ends[:, 1]
        starts[base] = chain(ends[:, 1], ends[:, 0], range(seqs), lambda k: k < seq, init[base:base + part])
        if base:
            cot_far.append(swap(tie(cot_rest[0], end_state), "doc", 2))
            kept[0] = tie(kept[0], cot_rest[0], w_out)
    dt_pre, delta = kept
    rank_in = rank_in.reshape(rows_all, rank)

    cot_all = jnp.concatenate([cot_top, cot_low, cot_near[0], cot_rest[0], cot_near[1], cot_rest[1], *cot_far], axis=0)
    cot_all = tie(cot_all, end_state)
    def relay_far(x):
        x, half = x.astype(BF), x.shape[0] // 32 * 16
        return swap(x[:half], "doc", 1), swap(x[half:], "doc", 2)

    def relay_near(parts, one, two):
        half = one.shape[0]
        first = jnp.concatenate([parts[1][:half], parts[1][half:] + two.astype(F32)], axis=0).astype(BF)
        second = jnp.concatenate([parts[2][:half] + one.astype(F32), parts[2][half:]], axis=0).astype(BF)
        return first, second

    d_start, skip_grad, out_rows = {}, [], {}
    kept = ()
    for base in (part, 0):
        rows = slice(base * tokens, (base + part) * tokens)
        d_gated = mm(cot_all[rows], w_out).reshape(part, tokens, block)
        if base == 0:
            d_gated = tie(d_gated, *out_rows.values())
        *kept, d_start[base], skip_part = forward(base, part, kept, delta, mixed, gate_in, d_gated, b_cols, c_diag, rate2,
                                                  starts[base], mask, skip)
        skip_grad.append(skip_part)
        for j in range(base + part - 1, base - 1, -1):
            out_rows[j] = mm_last(kept[2][j], w_out)
        if base:
            out_far = relay_far(out_rows[3])
    out_far = [tie(x, d_start[0]) for x in out_far]
    d_y, before, gated, d_gate, d_out = kept
    gated, d_gate = gated.reshape(rows_all, block), d_gate.reshape(rows_all, block)
    skip_grad = sum(jnp.sum(x, axis=(0, 1)) for x in skip_grad)
    later = lax.all_gather(jnp.concatenate([d_start[0], d_start[part]], axis=0).astype(BF), "seq")
    decays = jnp.concatenate([decays[0], decays[part]], axis=1)
    zero = jnp.zeros((docs, states, block), F32)
    back = range(seqs - 1, -1, -1)
    later_sum = chain(decays, later, back, lambda k: k > seq, zero)
    first_sum = chain(decays, later, back, lambda k: True, zero)

    def seq_sum(x):
        return lax.psum_scatter(x, "seq", scatter_dimension=0, tiled=True)

    def all_blocks(total):
        return lax.all_gather(total, "doc", axis=1, tiled=True)

    out_first, out_second = relay_near(out_rows, *out_far)
    out_got = swap(out_first, "doc", 1), swap(out_second, "doc", 2)
    gated = tie(gated, out_first, out_second)
    out_part = mm_first(cot_all, gated).astype(BF)
    gate_part = mm_first(normed, d_gate).astype(BF)
    later_sum = tie(later_sum, out_part, gate_part)
    out_part, gate_part = seq_sum(out_part), seq_sum(gate_part)

    d_out = d_out.reshape(docs, tokens, states)

    def proj_parts(kept, begin):
        rows = slice(begin, begin + middle)
        d_rank = mm_last(kept[0][:, rows].reshape(docs * middle, block), dt_full).reshape(docs, middle, rank)
        d_in = kept[2].reshape(docs, tokens, states)[:, rows]
        full = jnp.concatenate([d_rank, d_in, d_out[:, rows]], axis=2)
        return full[0], [full[j].astype(BF) for j in slots[1:]]

    def run_back(begin, kept, state):
        return backward(0, docs, begin, kept, dt_pre, delta, mixed, d_y, before, c_cols, b_diag, rate2, state, mask, skip)

    *kept, rate_grad, dt_bias_grad, passed_on = run_back(middle, (), later_sum)
    kept[0] = tie(kept[0], *out_got)
    out_got = [tie(x, kept[2]) for x in out_got]
    out_total = all_blocks(tie(out_part, kept[2]))
    own_late, sent = proj_parts(kept, middle)
    got = [swap(x, "doc", j) for j, x in zip(slots[1:], sent)]
    kept[0] = tie(kept[0], *sent)
    *kept, rate_part, bias_part, _ = run_back(0, kept, passed_on)
    got = [tie(x, kept[2]) for x in got]
    own_late = (own_late + sum(x.astype(F32) for x in got)).astype(BF)
    kept[0] = tie(kept[0], own_late, out_total)
    gate_total = all_blocks(tie(gate_part, kept[2]))
    late = [own_late] + [swap(own_late, "doc", j) for j in slots[1:]]
    d_pre, d_mix, _ = kept
    rate_grad = jnp.sum(rate_grad + rate_part, axis=0)
    dt_bias_grad = jnp.sum(dt_bias_grad + bias_part, axis=(0, 1))
    own_early, sent = proj_parts(kept, 0)
    got = [swap(x, "doc", j) for j, x in zip(slots[1:], sent)]

    nothing = jnp.zeros((docs, 8, block), F32)
    d_proj_late = tie(jnp.stack(late), *sent)
    d_inner, tail, carry, sums_late = conv_back(middle, (), nothing, d_proj_late, xproj_t, d_mix, inner_x, rim, conv_taps,
                                                conv_shift)
    d_gate = tie(d_gate, *sent).reshape(docs, tokens, block)
    gate_far = mm_last(d_gate[3], w_gate)
    own_early = (own_early + sum(x.astype(F32) for x in got)).astype(BF)
    d_inner = tie(d_inner, own_early)
    early = [own_early] + [swap(own_early, "doc", j) for j in slots[1:]]

    d_inner = tie(d_inner, gate_far, *early[1:])
    d_proj_early = jnp.stack(early)
    d_proj = jnp.concatenate([d_proj_early, d_proj_late], axis=1).reshape(rows_all, -1)
    few = jnp.concatenate([rate_grad, dt_bias_grad[None], skip_grad[None], jnp.zeros((14, block), F32)], axis=0)
    small_grad = [few, mm_first(rank_in, d_pre.reshape(rows_all, block)),
                  mm_first(d_proj, mixed_flat)]
    if near:
        side = seq % 2
        small_sum, sent = (jnp.concatenate([piece(x, at_side, block // 2, 1) for x in small_grad], axis=0)
                           for at_side in (side, 1 - side))
        small_sum = (small_sum + swap(sent.astype(BF), "seq", 1).astype(F32)).astype(BF)
        turned = lax.ppermute(small_sum, ("doc", "seq"), turn)
        d_proj_early = tie(d_proj_early, small_sum, gate_total)
    else:
        small_grad = jnp.concatenate(small_grad, axis=0)
        small_sum = lax.psum_scatter(small_grad, "seq", scatter_dimension=1, tiled=True)
        small_sum = lax.all_gather(small_sum.astype(BF), ("doc", "seq"), axis=1, tiled=True)
        turned = piece(small_sum, seq, inner // seqs, 1).astype(F32)

    d_inner, _, head, sums = conv_back(0, [d_inner], carry, d_proj_early, xproj_t, d_mix, inner_x, rim, conv_taps, conv_shift)
    d_ext = jnp.stack([sum(conv_taps[k] * head[:, j - k] for k in range(j + 1)) for j in range(lead)], axis=1)
    passed = shifted(d_ext.astype(BF), "seq", -1).astype(F32)
    d_inner = lax.dynamic_update_slice(d_inner, (tail[:, 8 - lead:] + passed).astype(BF), (0, tokens - lead, 0))
    d_inner = tie(d_inner, turned)
    inner_part = mm_first(normed, d_inner.reshape(rows_all, block)).astype(BF)
    d_inner = tie(d_inner, inner_part)
    inner_part = seq_sum(inner_part)
    small_sum = sum(x.astype(F32) for x in doc_gather(turned)) if near else turned
    d_inner = tie(d_inner, small_sum)

    d_gate = tie(d_gate, d_inner)

    def normed_part(j):
        return mm_last(d_inner[j], w_inner) + mm_last(d_gate[j], w_gate)

    far = mm_last(d_inner[3], w_inner) + gate_far
    far_got = relay_far(far)
    d_inner = tie(d_inner, far)
    parts = [normed_part(j) for j in range(3)]
    first, second = relay_near(parts, *(tie(x, parts[0]) for x in far_got))
    early_got = swap(first, "doc", 1), swap(second, "doc", 2)
    inner_total = all_blocks(tie(inner_part, first, second))
    gain = norm_gain.astype(F32)[:, None]
    in_total, gain_sum = place(doc[None], [], [gate_total], in_weight, gain, jnp.zeros((width // seqs, 128), F32), block, docs)

    output = (hidden.astype(F32) + out_rows[0] + sum(x.astype(F32) for x in out_got)).astype(BF)
    sums = jnp.sum((sums + sums_late).reshape(docs, taps + 1, 8, block), axis=(0, 2))
    ends = jnp.concatenate([jnp.where(seq == 0, tie(d_ext, *early_got, inner_part), 0.0).reshape(docs * lead, block), sums], axis=0)
    if near:
        for flip in (1, 2, 4):
            ends = ends + swap(ends, "seq", flip)
    else:
        ends = lax.psum(ends, "seq")
    sends = [jnp.concatenate([first_sum[j], ends[j * lead:(j + 1) * lead], ends[docs * lead:]], axis=0) for j in slots]
    ends = doc_place([sends[0]] + [swap(sends[j], "doc", j) for j in slots[1:]], doc, 1)
    init_grad, conv_sum = ends[:states + lead], piece(ends[states + lead:], seq, inner // seqs, 1)
    input_grad = input_gradient(parts[0], *early_got, hidden, cot)
    in_total, gain_sum = place(doc[None], [in_total], [inner_total], in_weight, gain, gain_sum, block, 0)
    gain_sum = jnp.sum(gain_sum, axis=1)

    return (
        output[None],
        input_grad[None],
        init_grad[None, :states],
        init_grad[None, states:],
        gain_sum,
        in_total,
        conv_sum[1:],
        conv_sum[0],
        small_sum[states + 16 + rank:].T,
        small_sum[states + 16:states + 16 + rank],
        small_sum[states],
        small_sum[:states],
        small_sum[states + 1],
        out_total.astype(F32),
    )


def solution(mesh):
    placed = (
        P("doc", "seq", None), P("doc", "seq", None), P("doc", None, None), P("doc", None, None),
        P("seq"), P("seq", None), P(None, "seq"), P("seq"), P("seq", None), P(None, "seq"),
        P("seq"), P(None, "seq"), P("seq"), P("seq", None),
    )
    return jax.shard_map(shards, mesh=mesh, in_specs=placed, out_specs=placed, check_vma=False)
```

time: 3740 us -> 821 us (0.22)
  other arithmetic: 1470 us -> 72.8 us
  waiting for transfers between devices: 1290 us -> 128 us
  local copies, waits for them, and re-layouts: 548 us -> 81.9 us
  Pallas kernels: 0 us -> 312 us
  blocking collectives: 151 us -> 0 us
  matrix products: 226 us -> 137 us
  starting transfers between devices: 4.55 us -> 68.6 us
    reduce_sum x1139 -> x7, other arithmetic: 1050 us -> 3.13 us  [the longest x1 1.58 us: shards(): gain_sum = jnp.sum(gain_sum, axis=1)]
    reduce_scatter x4 -> x3, waiting for transfers between devices: 820 us -> 0.04 us  [seq_sum(): return lax.psum_scatter(x, 'seq', scatter_dimension=0, tiled=True)]
    all_gather x8 -> x9, waiting for transfers between devices: 404 us -> 0.05 us  [the longest x1 0.02 us: shards(): lax.all_gather(jnp.concatenate([d_start[0], d_start[part]], axis=0).astyp...]
    slice x262 -> x40, local copies, waits for them, and re-layouts: 342 us -> 24 us  [the longest x2 3.23 us: relay_far(): return (swap(x[:half], 'doc', 1), swap(x[half:], 'doc', 2))]
    pallas_call x0 -> x61, Pallas kernels: none -> 312 us  [the longest x2 92.6 us: backward(): pl.pallas_call(backward_kernel, out_shape=[shape(delta.shape, BF), shape(...]
    dynamic_update_slice x128 -> x0, other arithmetic: 127 us -> none  [run_blocks(): lax.scan(jax.checkpoint(block_step), state_now, blocked)]
    ppermute x0 -> x55, waiting for transfers between devices: none -> 126 us  [the longest x49 126 us: swap(): lax.ppermute(x, axis, [(i, i ^ flip) for i in range(lax.axis_size(axis))])]
    all_gather x6 -> x0, blocking collectives: 106 us -> none  [the longest x1 27.9 us: shards(): lax.all_gather(conv_weight, 'seq', axis=1, tiled=True)]
  transfers between devices with their start and end apart: 17 -> 68, of which waited for: 8 -> 19; matrix products, arithmetic and copies ran while one was open for 15% -> 31% of each run, Pallas kernels for 0% -> 38%
where the time goes in v1:
time: 821 us; the launch traced here: 816 us
  Pallas kernels  312 us (38%)
  matrix products  137 us (17%)
  waiting for transfers between devices  128 us (16%)
  local copies, waits for them, and re-layouts  81.9 us (10%)
  other arithmetic  72.8 us (9%)
  starting transfers between devices  68.6 us (8%)
  between operations  16.3 us (2%)
    ppermute x49, waiting for transfers between devices, swap(): lax.ppermute(x, axis, [(i, i ^ flip) for i in range(lax.axis_size(axis))])  126 us
    pallas_call x2, Pallas kernels, backward(): pl.pallas_call(backward_kernel, out_shape=[shape(delta.shape, BF), shape(...  92.6 us
    pallas_call x2, Pallas kernels, forward(): pl.pallas_call(forward_kernel, out_shape=[shape(delta.shape), shape((docs...  85.3 us
    dot_general x14, matrix products, mm_last(): return lax.dot_general(a, b, LAST, preferred_element_type=F32)  59.5 us
    ppermute x49, starting transfers between devices, swap(): lax.ppermute(x, axis, [(i, i ^ flip) for i in range(lax.axis_size(axis))])  56.4 us
    pallas_call x2, Pallas kernels, summary(): pl.pallas_call(summary_kernel, out_shape=[shape((docs, tokens, width))] *...  49.2 us
    dot_general x5, matrix products, mm_first(): return lax.dot_general(a, b, FIRST, preferred_element_type=F32)  43.5 us
    pallas_call x4, Pallas kernels, front(): pl.pallas_call(functools.partial(front_kernel, lead=lead), out_shape=[sha...  40.8 us
  transfers between devices with their start and end apart: 68, of which 19 were waited for; matrix products, arithmetic and copies ran while one was open for 31% of the time, Pallas kernels for 38%

profile of v1, /device:TPU:0, one launch (start us, length us, event | category | flops | bytes accessed | tf_op | source)
XLA Modules:
  0.0 816.3 jit_solution(6408043142875300564)
XLA Ops:
  35.0 16.6 %collective-permute-done.7.refs_3_.top_ref = bf16[256,2048]{1,0:T(8,128)(2,1)} collective-permute-done((bf16[256,2048]{1,0:T(8,128)(2,1)}, bf16[256,2048]{1,0:T(8,128)(2,1)}, u32[]{:S(2)}, u32[]{:S(2)}) %collective-permute-start.7) | collective-permute-done | bytes 1048608 | tf_op jit(solution)/shard_map/ppermute | solution.py:478
  51.6 10.4 %collective-permute-done.5.refs_1_.top_ref = bf16[256,2048]{1,0:T(8,128)(2,1)S(1)} collective-permute-done((bf16[256,2048]{1,0:T(8,128)(2,1)}, bf16[256,2048]{1,0:T(8,128)(2,1)S(1)}, u32[]{:S(2)}, u32[]{:S(2)}) %collective-permute-start.5) | collective-permute-done | bytes 1048608 | tf_op jit(solution)/shard_map/ppermute | solution.py:478
  62.0 17.2 %collective-permute-done.8.refs_4_.low_ref = bf16[256,2048]{1,0:T(8,128)(2,1)} collective-permute-done((bf16[256,2048]{1,0:T(8,128)(2,1)}, bf16[256,2048]{1,0:T(8,128)(2,1)}, u32[]{:S(2)}, u32[]{:S(2)}) %collective-permute-start.8) | collective-permute-done | bytes 1048608 | tf_op jit(solution)/shard_map/ppermute | solution.py:478
  104.3 10.3 %front.4 = (bf16[2048,2048]{1,0:T(8,128)(2,1)}, f32[4,512,1024]{2,1,0:T(8,128)}, bf16[4,512,1024]{2,1,0:T(8,128)(2,1)}, f32[4,8,1024]{2,1,0:T(8,128)}, f32[512,160]{1,0:T(8,128)}) custom-call(s32[1]{0:T(128)} %bitcast.1.first_ref, bf16[256,2048]{1,0:T(8,128)(2,1)} %get-tuple-element.157.top_ref, bf16[256,2048]{1,0:T(8,128)(2,1)} %tie.46.low_ref, ...), custom_call_target="tpu_custom_call" | custom-call | flops 100000000 | tf_op jit(solution)/shard_map/front/pallas_call | solution.py:104
  114.6 10.1 %front.5 = (bf16[2048,2048]{1,0:T(8,128)(2,1)}, f32[4,512,1024]{2,1,0:T(8,128)}, bf16[4,512,1024]{2,1,0:T(8,128)(2,1)}, f32[4,8,1024]{2,1,0:T(8,128)}, f32[512,160]{1,0:T(8,128)}) custom-call(s32[1]{0:T(128)} %bitcast.1.first_ref, bf16[256,2048]{1,0:T(8,128)(2,1)} %copy-done.32, ...), custom_call_target="tpu_custom_call", output_to_operand_aliasing={{0}: (8, {}), {1}: (9, {}), {2}: (10, {}), {3}: (11, {})} | custom-call | flops 100000000 | tf_op jit(solution)/shard_map/front/pallas_call | solution.py:104
  124.7 10.2 %front.6 = (bf16[2048,2048]{1,0:T(8,128)(2,1)}, f32[4,512,1024]{2,1,0:T(8,128)}, bf16[4,512,1024]{2,1,0:T(8,128)(2,1)}, f32[4,8,1024]{2,1,0:T(8,128)}, f32[512,160]{1,0:T(8,128)}) custom-call(s32[1]{0:T(128)} %bitcast.1.first_ref, ...), custom_call_target="tpu_custom_call", output_to_operand_aliasing={{0}: (8, {}), {1}: (9, {}), {2}: (10, {}), {3}: (11, {})} | custom-call | flops 100000000 | tf_op jit(solution)/shard_map/front/pallas_call | solution.py:104
  138.9 10.2 %front.7 = (bf16[2048,2048]{1,0:T(8,128)(2,1)}, f32[4,512,1024]{2,1,0:T(8,128)}, bf16[4,512,1024]{2,1,0:T(8,128)(2,1)}, f32[4,8,1024]{2,1,0:T(8,128)}, f32[512,160]{1,0:T(8,128)}) custom-call(s32[1]{0:T(128)} %bitcast.1.first_ref, bf16[256,2048]{1,0:T(8,128)(2,1)} %tie.48.top_ref.refs_1_, ...), custom_call_target="tpu_custom_call", output_to_operand_aliasing={{0}: (8, {}), {1}: (9, {}), {2}: (10, {}), {3}: (11, {})} | custom-call | flops 100000000 | tf_op jit(solution)/shard_map/front/pallas_call | solution.py:104
  155.9 14.7 %fusion.116.refs_1_ = f32[2048,1024]{1,0:T(8,128)} fusion(bf16[2048,2048]{1,0:T(8,128)(2,1)} %get-tuple-element.92, bf16[2048,1024]{1,0:T(8,128)(2,1)} %tie.51), kind=kOutput, calls=%fused_computation.374 | convolution fusion | flops 8589934592 | bytes 20971520 | tf_op jit(solution)/shard_map/dot_general | solution.py:19
  200.9 24.6 %summary.2 = (f32[4,512,1024]{2,1,0:T(8,128)}, f32[4,512,1024]{2,1,0:T(8,128)}, f32[2,16,1024]{2,1,0:T(8,128)}, f32[2,16,1024]{2,1,0:T(8,128)}) custom-call(bf16[4,512,128]{2,1,0:T(8,128)(2,1)} %bitcast.510, bf16[128,1024]{1,0:T(8,128)(2,1)} %fusion.48.dtw_ref, f32[1,1024]{1,0:T(1,128)} %get-tuple-element.163.shift_ref, ...), custom_call_target="tpu_custom_call" | custom-call | flops 22000001024 | tf_op jit(solution)/shard_map/summary/pallas_call | solution.py:162
  236.5 24.5 %summary.3 = (f32[4,512,1024]{2,1,0:T(8,128)}, f32[4,512,1024]{2,1,0:T(8,128)}, f32[2,16,1024]{2,1,0:T(8,128)}, f32[2,16,1024]{2,1,0:T(8,128)}) custom-call(bf16[4,512,128]{2,1,0:T(8,128)(2,1)} %bitcast.511, bf16[128,1024]{1,0:T(8,128)(2,1)} %fusion.48.dtw_ref, ...), custom_call_target="tpu_custom_call", output_to_operand_aliasing={{0}: (6, {}), {1}: (7, {})} | custom-call | flops 22000001024 | tf_op jit(solution)/shard_map/summary/pallas_call | solution.py:162
  274.0 10.0 %fusion = f32[1024,1024]{1,0:T(8,128)} fusion(bf16[2048,1024]{1,0:T(8,128)(2,1)} %all-gather.14.cloned.1.call-done.refs_2_, bf16[2048,2048]{1,0:T(8,128)(2,1)} %tie.62), kind=kOutput, calls=%fused_computation.1 | convolution fusion | flops 4294967296 | bytes 12582912 | tf_op jit(solution)/shard_map/dot_general | solution.py:19
  284.0 43.0 %forward.2 = (f32[4,512,1024]{2,1,0:T(8,128)}, bf16[4,8192,1024]{2,1,0:T(8,128)(2,1)}, bf16[4,512,1024]{2,1,0:T(8,128)(2,1)}, bf16[4,512,1024]{2,1,0:T(8,128)(2,...) custom-call(f32[4,512,1024]{2,1,0:T(8,128)} %get-tuple-element.98.delta_ref, ...), custom_call_target="tpu_custom_call" | custom-call | flops 44999999488 | tf_op jit(solution)/shard_map/forward/pallas_call | solution.py:246
  351.4 42.3 %forward.3 = (f32[4,512,1024]{2,1,0:T(8,128)}, bf16[4,8192,1024]{2,1,0:T(8,128)(2,1)}, bf16[4,512,1024]{2,1,0:T(8,128)(2,1)}, bf16[4,512,1024]{2,1,0:T(8,128)(2,...) custom-call(f32[4,512,1024]{2,1,0:T(8,128)} %get-tuple-element.98.de, ...), custom_call_target="tpu_custom_call", output_to_operand_aliasing={{0}: (10, {}), {1}: (11, {}), {2}: (12, {}), {3}: (13, {}),... | custom-call | flops 44999999488 | tf_op jit(solution)/shard_map/forward/pallas_call | solution.py:246
  419.1 14.0 %convolution_convert_fusion.2.refs_1_ = bf16[2048,1024]{1,0:T(8,128)(2,1)} fusion(bf16[2048,2048]{1,0:T(8,128)(2,1)} %tie.62, bf16[2048,1024]{1,0:T(8,128)(2,1)} %tie.66), kind=kOutput, calls=%fused_computation.8 | convolution fusion | flops 8592031744 | bytes 16777216 | tf_op jit(solution)/shard_map/dot_general | solution.py:27
  433.4 14.0 %convolution_convert_fusion.1.refs_2_ = bf16[2048,1024]{1,0:T(8,128)(2,1)} fusion(bf16[2048,2048]{1,0:T(8,128)(2,1)} %get-tuple-element.92, bf16[2048,1024]{1,0:T(8,128)(2,1)} %bitcast.482), kind=kOutput, calls=%fused_computation.7 | convolution fusion | flops 8592031744 | bytes 16777216 | tf_op jit(solution)/shard_map/dot_general | solution.py:27
  459.7 46.4 %backward.2 = (bf16[4,512,1024]{2,1,0:T(8,128)(2,1)}, f32[4,512,1024]{2,1,0:T(8,128)}, f32[4,32,1,256]{3,2,1,0:T(1,128)}, f32[4,16,1024]{2,1,0:T(8,128)}, f32[4,...) custom-call(f32[4,512,1024]{2,1,0:T(8,128)} %get-tuple-element.110.pre_ref, f32[4,512,1024]{2,1,0:T(8,128)} %get-tuple-element.98.delta_ref, ...), custom_call_target="tpu_custom_call" | custom-call | flops 4000000000 | tf_op jit(solution)/shard_map/backward/pallas_call | solution.py:331
  521.7 46.2 %backward.3 = (bf16[4,512,1024]{2,1,0:T(8,128)(2,1)}, f32[4,512,1024]{2,1,0:T(8,128)}, f32[4,32,1,256]{3,2,1,0:T(1,128)}, f32[4,16,1024]{2,1,0:T(8,128)}, f32[4,...) custom-call(f32[4,512,1024]{2,1,0:T(8,128)} %get-tuple-element.110.pre_ref, ...), custom_call_target="tpu_custom_call", output_to_operand_aliasing={{0}: (11, {}), {1}: (12, {}), {2}: (13, {})} | custom-call | flops 4000000000 | tf_op jit(solution)/shard_map/backward/pallas_call | solution.py:331
  589.3 7.4 fusion.16.refs_1_
  598.1 13.4 %conv_back.2 = (bf16[4,512,1024]{2,1,0:T(8,128)(2,1)}, f32[4,8,1024]{2,1,0:T(8,128)}, f32[4,8,1024]{2,1,0:T(8,128)}, f32[4,40,1024]{2,1,0:T(8,128)}) custom-call(bf16[4,256,160]{2,1,0:T(8,128)(2,1)} %tie.77.dproj_ref, bf16[160,1024]{1,0:T(8,128)(2,1)} %fusion.40.xproj_ref, f32[4,512,1024]{2,1,0:T(8,128)} %get-tuple-element.128.dmix_ref, ...), custom_call_target="tpu_custom_call" | custom-call | flops 200000000 | tf_op jit(solution)/shard_map/conv_back/pallas_call | solution.py:401
  623.8 13.0 %conv_back.3 = (bf16[4,512,1024]{2,1,0:T(8,128)(2,1)}, f32[4,8,1024]{2,1,0:T(8,128)}, f32[4,8,1024]{2,1,0:T(8,128)}, f32[4,40,1024]{2,1,0:T(8,128)}) custom-call(bf16[4,256,160]{2,1,0:T(8,128)(2,1)} %tie.79.dproj_ref, bf16[160,1024]{1,0:T(8,128)(2,1)} %fusion.40.xproj_ref, ...), custom_call_target="tpu_custom_call", output_to_operand_aliasing={{0}: (9, {})} | custom-call | flops 200000000 | tf_op jit(solution)/shard_map/conv_back/pallas_call | solution.py:401
  651.8 14.0 %convolution_convert_fusion.refs_1_ = bf16[2048,1024]{1,0:T(8,128)(2,1)} fusion(bf16[2048,2048]{1,0:T(8,128)(2,1)} %get-tuple-element.92, bf16[2048,1024]{1,0:T(8,128)(2,1)} %bitcast.477), kind=kOutput, calls=%fused_computation.6 | convolution fusion | flops 8592031744 | bytes 16777216 | tf_op jit(solution)/shard_map/dot_general | solution.py:27
  667.8 8.2 %fusion.115 = (bf16[512,2048]{1,0:T(8,128)(2,1)S(1)}, f32[512,2048]{1,0:T(8,128)}) fusion(f32[512,2048]{1,0:T(8,128)} %fusion.16.refs_1_, bf16[2048,1024]{1,0:T(8,128)(2,1)} %all-gather.10.cloned.1.call-done.w_ref, bf16[4,512,1024]{2,1,0:T(8,128)(2,1)} %tie.85.refs_0_.refs_1_), kind=kOutput, calls=%fused_computation.373 | convolution fusion | flops 2149580800 | bytes 15728640 | tf_op jit(solution)/shard_map/dot_general | solution.py:23
  716.8 38.8 %collective-permute-done.47.one_ref.refs_1_ = bf16[512,2048]{1,0:T(8,128)(2,1)} collective-permute-done((bf16[512,2048]{1,0:T(8,128)(2,1)S(1)}, bf16[512,2048]{1,0:T(8,128)(2,1)}, u32[]{:S(2)}, u32[]{:S(2)}) %collective-permute-start.47) | collective-permute-done | bytes 2097184 | tf_op jit(solution)/shard_map/ppermute | solution.py:478
  791.9 7.8 input_gradient.1
  (608 shorter events, 332.9 us)
Async XLA Ops:
  7.2 97.1 %all-gather.10.cloned.1.call-start = ((), (), s32[]{:S(2)}) async-start(), calls=%async_computation.3 | async-start | bytes 4718592 | tf_op jit(solution)/shard_map/all_gather | solution.py:534
  12.4 143.5 %all-gather.12.cloned.1.call-start = ((), (), s32[]{:S(2)}) async-start(), calls=%async_computation.4 | async-start | bytes 4718592 | tf_op jit(solution)/shard_map/all_gather | solution.py:534
  28.5 50.6 %collective-permute-start.8 = (bf16[256,2048]{1,0:T(8,128)(2,1)}, bf16[256,2048]{1,0:T(8,128)(2,1)}, u32[]{:S(2)}, u32[]{:S(2)}) collective-permute-start(bf16[256,2048]{1,0:T(8,128)(2,1)} %tie.46.low_ref), channel_id=1, source_target_pairs={{0,16},{8,24},{16,0},{24,8},{1,17},{9,25},{17,1},{25,9},{2,18},{10... | collective-permute-start | bytes 3145736 | tf_op jit(solution)/shard_map/ppermute | solution.py:478
  29.0 57.1 %collective-permute-start.6 = (bf16[256,2048]{1,0:T(8,128)(2,1)}, bf16[256,2048]{1,0:T(8,128)(2,1)}, u32[]{:S(2)}, u32[]{:S(2)}) collective-permute-start(bf16[256,2048]{1,0:T(8,128)(2,1)} %tie.46.low_ref), channel_id=1, source_target_pairs={{0,8},{8,0},{16,24},{24,16},{1,9},{9,1},{17,25},{25,17},{2,10},{10... | collective-permute-start | bytes 3145736 | tf_op jit(solution)/shard_map/ppermute | solution.py:478
  90.6 144.8 %all-gather.14.cloned.1.call-start = ((), (), s32[]{:S(2)}) async-start(), calls=%async_computation.5 | async-start | bytes 4718592 | tf_op jit(solution)/shard_map/all_gather | solution.py:534
  91.5 172.9 %all-gather.16.cloned.1.call-start = ((), (), s32[]{:S(2)}) async-start(), calls=%async_computation.6 | async-start | bytes 1179648 | tf_op jit(solution)/shard_map/all_gather | solution.py:629
  136.9 55.2 %collective-permute-start.19 = (bf16[256,2048]{1,0:T(8,128)(2,1)}, bf16[256,2048]{1,0:T(8,128)(2,1)S(1)}, u32[]{:S(2)}, u32[]{:S(2)}) collective-permute-start(bf16[256,2048]{1,0:T(8,128)(2,1)} %tie.55), channel_id=1, source_target_pairs={{0,16},{8,24},{16,0},{24,8},{1,17},{9,25},{17,1},{25,9},{2,18},{10... | collective-permute-start | bytes 3145736 | tf_op jit(solution)/shard_map/ppermute | solution.py:478
  138.9 53.1 %collective-permute-start.18 = (bf16[256,2048]{1,0:T(8,128)(2,1)}, bf16[256,2048]{1,0:T(8,128)(2,1)S(1)}, u32[]{:S(2)}, u32[]{:S(2)}) collective-permute-start(bf16[256,2048]{1,0:T(8,128)(2,1)} %tie.55), channel_id=1, source_target_pairs={{0,8},{8,0},{16,24},{24,16},{1,9},{9,1},{17,25},{25,17},{2,10},{10... | collective-permute-start | bytes 3145736 | tf_op jit(solution)/shard_map/ppermute | solution.py:478
  196.0 66.0 %collective-permute-start.21 = (bf16[256,2048]{1,0:T(8,128)(2,1)}, bf16[256,2048]{1,0:T(8,128)(2,1)}, u32[]{:S(2)}, u32[]{:S(2)}) collective-permute-start(bf16[256,2048]{1,0:T(8,128)(2,1)} %tie.57), channel_id=1, source_target_pairs={{0,16},{8,24},{16,0},{24,8},{1,17},{9,25},{17,1},{25,9},{2,18},{10... | collective-permute-start | bytes 3145736 | tf_op jit(solution)/shard_map/ppermute | solution.py:478
  227.2 122.1 %all-gather.18.cloned.1.call-start = ((), (), s32[]{:S(2)}) async-start(), calls=%async_computation.7 | async-start | bytes 1179648 | tf_op jit(solution)/shard_map/all_gather | solution.py:629
  274.0 181.0 %all-gather.20.cloned.1.call-start = ((), (), s32[]{:S(2)}) async-start(), calls=%async_computation.8 | async-start | bytes 1179648 | tf_op jit(solution)/shard_map/all_gather | solution.py:668
  340.4 66.3 %collective-permute-start.24 = (bf16[256,2048]{1,0:T(8,128)(2,1)}, bf16[256,2048]{1,0:T(8,128)(2,1)S(1)}, u32[]{:S(2)}, u32[]{:S(2)}) collective-permute-start(bf16[256,2048]{1,0:T(8,128)(2,1)} %get-tuple-element.152), channel_id=1, source_target_pairs={{0,16},{8,24},{16,0},{24,8},{1,17},{9,25},{17,1},{25,9},{2,18},{10... | collective-permute-start | bytes 3145736 | tf_op jit(solution)/shard_map/ppermute | solution.py:478
  341.2 62.3 %collective-permute-start.26 = (bf16[256,2048]{1,0:T(8,128)(2,1)}, bf16[256,2048]{1,0:T(8,128)(2,1)S(1)}, u32[]{:S(2)}, u32[]{:S(2)}) collective-permute-start(bf16[256,2048]{1,0:T(8,128)(2,1)} %get-tuple-element.153), channel_id=1, source_target_pairs={{0,8},{8,0},{16,24},{24,16},{1,9},{9,1},{17,25},{25,17},{2,10},{10... | collective-permute-start | bytes 3145736 | tf_op jit(solution)/shard_map/ppermute | solution.py:478
  395.3 110.8 %reduce-scatter.4.cloned.1.call-start = ((), (), s32[]{:S(2)}) async-start(), calls=%async_computation.9 | async-start | bytes 4718592 | tf_op jit(solution)/shard_map/reduce_scatter | solution.py:676
  433.1 143.1 %reduce-scatter.6.cloned.1.call-start = ((), (), s32[]{:S(2)}) async-start(), calls=%async_computation.11 | async-start | bytes 4718592 | tf_op jit(solution)/shard_map/reduce_scatter | solution.py:676
  447.4 134.0 %all-gather.22.cloned.1.call-start = ((), (), s32[]{:S(2)}) async-start(), calls=%async_computation.10 | async-start | bytes 2621440 | tf_op jit(solution)/shard_map/all_gather | solution.py:679
  451.7 60.0 %collective-permute-start.27 = (bf16[512,2048]{1,0:T(8,128)(2,1)}, bf16[512,2048]{1,0:T(8,128)(2,1)S(1)}, u32[]{:S(2)}, u32[]{:S(2)}) collective-permute-start(bf16[512,2048]{1,0:T(8,128)(2,1)} %pad_maximum_fusion.1.refs_2_), channel_id=1, source_target_pairs={{0,16},{8,24},{16,0},{24,8},{1,17},{9,25},{17,1},{25,9},{2,18},{10... | collective-permute-start | bytes 6291464 | tf_op jit(solution)/shard_map/ppermute | solution.py:478
  452.4 59.4 %collective-permute-start.25 = (bf16[512,2048]{1,0:T(8,128)(2,1)}, bf16[512,2048]{1,0:T(8,128)(2,1)}, u32[]{:S(2)}, u32[]{:S(2)}) collective-permute-start(bf16[512,2048]{1,0:T(8,128)(2,1)} %pad_maximum_fusion.refs_1_), channel_id=1, source_target_pairs={{0,8},{8,0},{16,24},{24,16},{1,9},{9,1},{17,25},{25,17},{2,10},{10... | collective-permute-start | bytes 6291464 | tf_op jit(solution)/shard_map/ppermute | solution.py:478
  506.2 117.6 %all-gather.24.cloned.1.call-start = ((), (), s32[]{:S(2)}) async-start(), calls=%async_computation.12 | async-start | bytes 2621440 | tf_op jit(solution)/shard_map/all_gather | solution.py:679
  517.2 52.0 %collective-permute-start.30 = (bf16[256,160]{1,0:T(8,128)(2,1)S(1)}, bf16[256,160]{1,0:T(8,128)(2,1)S(1)}, u32[]{:S(2)}, u32[]{:S(2)}) collective-permute-start(bf16[256,160]{1,0:T(8,128)(2,1)S(1)} %get-tuple-element.177.refs_3_), channel_id=1, source_target_pairs={{0,24},{8,16},{16,8},{24,0},{1,25},{9,17},{17,9},{25,1},{2,26},{10... | collective-permute-start | bytes 245768 | tf_op jit(solution)/shard_map/ppermute | solution.py:478
  518.7 51.2 %collective-permute-start.29 = (bf16[256,160]{1,0:T(8,128)(2,1)S(1)}, bf16[256,160]{1,0:T(8,128)(2,1)S(1)}, u32[]{:S(2)}, u32[]{:S(2)}) collective-permute-start(bf16[256,160]{1,0:T(8,128)(2,1)S(1)} %get-tuple-element.178.refs_2_), channel_id=1, source_target_pairs={{0,16},{8,24},{16,0},{24,8},{1,17},{9,25},{17,1},{25,9},{2,18},{10... | collective-permute-start | bytes 245768 | tf_op jit(solution)/shard_map/ppermute | solution.py:478
  520.2 50.4 %collective-permute-start.28 = (bf16[256,160]{1,0:T(8,128)(2,1)S(1)}, bf16[256,160]{1,0:T(8,128)(2,1)S(1)}, u32[]{:S(2)}, u32[]{:S(2)}) collective-permute-start(bf16[256,160]{1,0:T(8,128)(2,1)S(1)} %copy-done.68), channel_id=1, source_target_pairs={{0,8},{8,0},{16,24},{24,16},{1,9},{9,1},{17,25},{25,17},{2,10},{10... | collective-permute-start | bytes 245768 | tf_op jit(solution)/shard_map/ppermute | solution.py:478
  576.4 184.6 %reduce-scatter.8.cloned.1.call-start = ((), (), s32[]{:S(2)}) async-start(), calls=%async_computation.13 | async-start | bytes 4718592 | tf_op jit(solution)/shard_map/reduce_scatter | solution.py:676
  712.9 48.1 %collective-permute-start.49 = (bf16[512,2048]{1,0:T(8,128)(2,1)}, bf16[512,2048]{1,0:T(8,128)(2,1)}, u32[]{:S(2)}, u32[]{:S(2)}) collective-permute-start(bf16[512,2048]{1,0:T(8,128)(2,1)} %pad_maximum_fusion.3.refs_2_), channel_id=1, source_target_pairs={{0,16},{8,24},{16,0},{24,8},{1,17},{9,25},{17,1},{25,9},{2,18},{10... | collective-permute-start | bytes 6291464 | tf_op jit(solution)/shard_map/ppermute | solution.py:478
  (155 other events, 2063.3 us)
Sparse Core Ops, SparseCore 0:
  12.5 70.5 all-gather.9
  90.7 46.6 all-gather.11
  138.9 45.8 all-gather.13
  227.4 20.7 all-gather.15
  274.1 20.5 all-gather.17
  395.4 20.6 all-gather.19
  433.3 48.4 reduce-scatter.3
  484.1 48.0 reduce-scatter.5
  534.1 33.5 all-gather.21
  576.5 39.2 all-gather.23
  665.9 50.4 reduce-scatter.7
  763.4 36.7 all-gather.25

commit v2 on v1

--- a/solution.py
+++ b/solution.py
@@ -123,10 +123,11 @@
     pre_ref, delta_ref, end_ref, decay_ref = refs[-4:]
     tokens, width = mixed_ref.shape[1:]
     rate = rate_ref[...]
-    count = tokens // TB
+    group = 4
+    count = tokens // (TB * group)
 
     def steps(i):
-        rows = pl.ds(pl.multiple_of(i * TB, TB), TB)
+        rows = pl.ds(pl.multiple_of(i * TB * group, TB * group), TB * group)
         pre = mm(rank_ref[0, rows], dtw_ref[...]) + shift_ref[...]
         pre_ref[0, rows] = pre
         delta_ref[0, rows] = softplus(pre)
@@ -135,14 +136,16 @@
 
     def body(i, carry):
         h, total = carry
-        rows = pl.ds(pl.multiple_of(i * TB, TB), TB)
-        dl = delta_ref[0, rows]
-        dr = dl * mixed_ref[0, rows].astype(F32)
-        bt = bt_ref[0, i]
-        for t in range(TB):
-            h = jnp.exp2(dl[t:t + 1] * rate) * h + bt[:, t:t + 1] * dr[t:t + 1]
+        for b in range(group):
+            rows = pl.ds(pl.multiple_of((i * group + b) * TB, TB), TB)
+            dl = delta_ref[0, rows]
+            dr = dl * mixed_ref[0, rows].astype(F32)
+            bt = bt_ref[0, i * group + b]
+            for t in range(TB):
+                h = jnp.exp2(dl[t:t + 1] * rate) * h + bt[:, t:t + 1] * dr[t:t + 1]
+            total = total + dl
         steps(jnp.minimum(i + 1, count - 1))
-        return h, total + dl
+        return h, total
 
     h, total = lax.fori_loop(0, count, body, (jnp.zeros(rate.shape, F32), jnp.zeros((TB, width), F32)))
     end_ref[0] = h
@@ -172,7 +175,7 @@
 
 def forward_kernel(delta_ref, mixed_ref, gate_ref, dg_ref, bt_ref, cdiag_ref, rate_ref, start_ref, mask_ref, skip_ref,
                    *refs):
-    dy_ref, before_ref, gated_ref, dgate_ref, dout_ref, dstart_ref, sgrad_ref, hs_ref, ps_ref, hb_ref, zb_ref, sb_ref = refs[-12:]
+    dy_ref, before_ref, gated_ref, dgate_ref, dout_ref, dstart_ref, sgrad_ref, hs_ref, ps_ref, hb_ref, zb_ref, sb_ref, sig_ref = refs[-13:]
     tokens = delta_ref.shape[1]
     n = rate_ref.shape[0]
     count = tokens // TB
@@ -190,13 +193,9 @@
 
     def finish(i, hm, good):
         rows = pl.ds(pl.multiple_of(i * TB, TB), TB)
-        gate, dg = gate_ref[0, rows], dg_ref[0, rows]
-        sig = sigmoid(gate)
+        gate, dg, sig = gate_ref[0, rows], dg_ref[0, rows], sig_ref[...]
         act = gate * sig
         mx = mixed_ref[0, rows].astype(F32)
-        dy = dg * act
-        dy_ref[0, rows] = dy
-        sgrad_ref[0] += jnp.where(good, dy * mx, 0.0)
         y = mm(cdiag_ref[0, i], hm) + skip_ref[...] * mx
         gated_ref[0, rows] = (y * act).astype(BF)
         dgate_ref[0, rows] = (dg * y * (sig * (1.0 + gate * (1.0 - sig)))).astype(BF)
@@ -208,14 +207,19 @@
         h, p = carry
         rows = pl.ds(pl.multiple_of(i * TB, TB), TB)
         dl = delta_ref[0, rows]
-        dr = dl * mixed_ref[0, rows].astype(F32)
+        mx = mixed_ref[0, rows].astype(F32)
+        dr = dl * mx
         gate = gate_ref[0, rows]
-        dy = dg_ref[0, rows] * gate * sigmoid(gate)
+        sig = sigmoid(gate)
+        dy = dg_ref[0, rows] * (gate * sig)
+        dy_ref[0, rows] = dy
+        sgrad_ref[0] += dy * mx
         bt = bt_ref[0, i]
         hb = h.astype(BF)
         before_ref[0, pl.ds(pl.multiple_of(i * TB * n, TB * n), n)] = hb
         last = jnp.maximum(i - 1, 0)
         finish(last, before_ref[0, pl.ds(pl.multiple_of((last * TB + 1) * n, n), TB * n)], i > 0)
+        sig_ref[...] = sig
         for t in range(TB):
             if t:
                 before_ref[0, pl.ds(pl.multiple_of((i * TB + t) * n, n), n)] = hb
@@ -254,7 +258,7 @@
                    pl.BlockSpec((1, nb, 1, TB * n), lambda g, k: (g + base, k, 0, 0)), state,
                    pl.BlockSpec((1, TB, width), lambda g, k: (g, 0, 0))],
         scratch_shapes=[pltpu.VMEM((n, width), F32), pltpu.VMEM((n, width), F32), pltpu.VMEM((TB * n, width), BF),
-                        pltpu.VMEM((TB * n, width), BF), pltpu.VMEM((TB * n, 128), BF)],
+                        pltpu.VMEM((TB * n, width), BF), pltpu.VMEM((TB * n, 128), BF), pltpu.VMEM((TB, width), F32)],
         input_output_aliases=alias, compiler_params=params(), cost_estimate=cost(45), name="forward",
     )(delta, mixed, gate, d_gated, bt, cdiag, rate, start, mask, skip, *kept)
 

time: 821 us -> 815 us (level)
  transfers between devices with their start and end apart: 68 -> 68, of which waited for: 19 -> 19; matrix products, arithmetic and copies ran while one was open for 31% -> 31% of each run, Pallas kernels for 38% -> 37%
where the time goes in v2:
time: 815 us; the launch traced here: 810 us
  Pallas kernels  306 us (38%)
  matrix products  137 us (17%)
  waiting for transfers between devices  128 us (16%)
  local copies, waits for them, and re-layouts  81.9 us (10%)
  other arithmetic  72.8 us (9%)
  starting transfers between devices  68.6 us (8%)
  between operations  16.3 us (2%)
    ppermute x49, waiting for transfers between devices, swap(): lax.ppermute(x, axis, [(i, i ^ flip) for i in range(lax.axis_size(axis))])  126 us
    pallas_call x2, Pallas kernels, backward(): pl.pallas_call(backward_kernel, out_shape=[shape(delta.shape, BF), shape(...  92.6 us
    pallas_call x2, Pallas kernels, forward(): pl.pallas_call(forward_kernel, out_shape=[shape(delta.shape), shape((docs...  83.9 us
    dot_general x14, matrix products, mm_last(): return lax.dot_general(a, b, LAST, preferred_element_type=F32)  59.5 us
    ppermute x49, starting transfers between devices, swap(): lax.ppermute(x, axis, [(i, i ^ flip) for i in range(lax.axis_size(axis))])  56.4 us
    pallas_call x2, Pallas kernels, summary(): pl.pallas_call(summary_kernel, out_shape=[shape((docs, tokens, width))] *...  44.1 us
    dot_general x5, matrix products, mm_first(): return lax.dot_general(a, b, FIRST, preferred_element_type=F32)  43.5 us
    pallas_call x4, Pallas kernels, front(): pl.pallas_call(functools.partial(front_kernel, lead=lead), out_shape=[sha...  40.8 us
  transfers between devices with their start and end apart: 68, of which 19 were waited for; matrix products, arithmetic and copies ran while one was open for 31% of the time, Pallas kernels for 37%

profile of v2, /device:TPU:0, one launch (start us, length us, event | category | flops | bytes accessed | tf_op | source)
XLA Modules:
  0.0 809.9 jit_solution(7834092922924843767)
XLA Ops:
  35.0 16.6 %collective-permute-done.7.refs_3_.top_ref = bf16[256,2048]{1,0:T(8,128)(2,1)} collective-permute-done((bf16[256,2048]{1,0:T(8,128)(2,1)}, bf16[256,2048]{1,0:T(8,128)(2,1)}, u32[]{:S(2)}, u32[]{:S(2)}) %collective-permute-start.7) | collective-permute-done | bytes 1048608 | tf_op jit(solution)/shard_map/ppermute | solution.py:482
  51.6 10.4 %collective-permute-done.5.refs_1_.top_ref = bf16[256,2048]{1,0:T(8,128)(2,1)S(1)} collective-permute-done((bf16[256,2048]{1,0:T(8,128)(2,1)}, bf16[256,2048]{1,0:T(8,128)(2,1)S(1)}, u32[]{:S(2)}, u32[]{:S(2)}) %collective-permute-start.5) | collective-permute-done | bytes 1048608 | tf_op jit(solution)/shard_map/ppermute | solution.py:482
  62.0 17.2 %collective-permute-done.8.refs_4_.low_ref = bf16[256,2048]{1,0:T(8,128)(2,1)} collective-permute-done((bf16[256,2048]{1,0:T(8,128)(2,1)}, bf16[256,2048]{1,0:T(8,128)(2,1)}, u32[]{:S(2)}, u32[]{:S(2)}) %collective-permute-start.8) | collective-permute-done | bytes 1048608 | tf_op jit(solution)/shard_map/ppermute | solution.py:482
  104.3 10.3 %front.4 = (bf16[2048,2048]{1,0:T(8,128)(2,1)}, f32[4,512,1024]{2,1,0:T(8,128)}, bf16[4,512,1024]{2,1,0:T(8,128)(2,1)}, f32[4,8,1024]{2,1,0:T(8,128)}, f32[512,160]{1,0:T(8,128)}) custom-call(s32[1]{0:T(128)} %bitcast.1.first_ref, bf16[256,2048]{1,0:T(8,128)(2,1)} %get-tuple-element.157.top_ref, bf16[256,2048]{1,0:T(8,128)(2,1)} %tie.46.low_ref, ...), custom_call_target="tpu_custom_call" | custom-call | flops 100000000 | tf_op jit(solution)/shard_map/front/pallas_call | solution.py:104
  114.6 10.1 %front.5 = (bf16[2048,2048]{1,0:T(8,128)(2,1)}, f32[4,512,1024]{2,1,0:T(8,128)}, bf16[4,512,1024]{2,1,0:T(8,128)(2,1)}, f32[4,8,1024]{2,1,0:T(8,128)}, f32[512,160]{1,0:T(8,128)}) custom-call(s32[1]{0:T(128)} %bitcast.1.first_ref, bf16[256,2048]{1,0:T(8,128)(2,1)} %copy-done.32, ...), custom_call_target="tpu_custom_call", output_to_operand_aliasing={{0}: (8, {}), {1}: (9, {}), {2}: (10, {}), {3}: (11, {})} | custom-call | flops 100000000 | tf_op jit(solution)/shard_map/front/pallas_call | solution.py:104
  124.7 10.2 %front.6 = (bf16[2048,2048]{1,0:T(8,128)(2,1)}, f32[4,512,1024]{2,1,0:T(8,128)}, bf16[4,512,1024]{2,1,0:T(8,128)(2,1)}, f32[4,8,1024]{2,1,0:T(8,128)}, f32[512,160]{1,0:T(8,128)}) custom-call(s32[1]{0:T(128)} %bitcast.1.first_ref, ...), custom_call_target="tpu_custom_call", output_to_operand_aliasing={{0}: (8, {}), {1}: (9, {}), {2}: (10, {}), {3}: (11, {})} | custom-call | flops 100000000 | tf_op jit(solution)/shard_map/front/pallas_call | solution.py:104
  138.9 10.2 %front.7 = (bf16[2048,2048]{1,0:T(8,128)(2,1)}, f32[4,512,1024]{2,1,0:T(8,128)}, bf16[4,512,1024]{2,1,0:T(8,128)(2,1)}, f32[4,8,1024]{2,1,0:T(8,128)}, f32[512,160]{1,0:T(8,128)}) custom-call(s32[1]{0:T(128)} %bitcast.1.first_ref, bf16[256,2048]{1,0:T(8,128)(2,1)} %tie.48.top_ref.refs_1_, ...), custom_call_target="tpu_custom_call", output_to_operand_aliasing={{0}: (8, {}), {1}: (9, {}), {2}: (10, {}), {3}: (11, {})} | custom-call | flops 100000000 | tf_op jit(solution)/shard_map/front/pallas_call | solution.py:104
  155.9 14.7 %fusion.116.refs_1_ = f32[2048,1024]{1,0:T(8,128)} fusion(bf16[2048,2048]{1,0:T(8,128)(2,1)} %get-tuple-element.92, bf16[2048,1024]{1,0:T(8,128)(2,1)} %tie.51), kind=kOutput, calls=%fused_computation.374 | convolution fusion | flops 8589934592 | bytes 20971520 | tf_op jit(solution)/shard_map/dot_general | solution.py:19
  200.9 22.1 %summary.2 = (f32[4,512,1024]{2,1,0:T(8,128)}, f32[4,512,1024]{2,1,0:T(8,128)}, f32[2,16,1024]{2,1,0:T(8,128)}, f32[2,16,1024]{2,1,0:T(8,128)}) custom-call(bf16[4,512,128]{2,1,0:T(8,128)(2,1)} %bitcast.510, bf16[128,1024]{1,0:T(8,128)(2,1)} %fusion.48.dtw_ref, f32[1,1024]{1,0:T(1,128)} %get-tuple-element.163.shift_ref, ...), custom_call_target="tpu_custom_call" | custom-call | flops 22000001024 | tf_op jit(solution)/shard_map/summary/pallas_call | solution.py:165
  234.0 22.0 %summary.3 = (f32[4,512,1024]{2,1,0:T(8,128)}, f32[4,512,1024]{2,1,0:T(8,128)}, f32[2,16,1024]{2,1,0:T(8,128)}, f32[2,16,1024]{2,1,0:T(8,128)}) custom-call(bf16[4,512,128]{2,1,0:T(8,128)(2,1)} %bitcast.511, bf16[128,1024]{1,0:T(8,128)(2,1)} %fusion.48.dtw_ref, ...), custom_call_target="tpu_custom_call", output_to_operand_aliasing={{0}: (6, {}), {1}: (7, {})} | custom-call | flops 22000001024 | tf_op jit(solution)/shard_map/summary/pallas_call | solution.py:165
  269.0 10.0 %fusion = f32[1024,1024]{1,0:T(8,128)} fusion(bf16[2048,1024]{1,0:T(8,128)(2,1)} %all-gather.14.cloned.1.call-done.refs_2_, bf16[2048,2048]{1,0:T(8,128)(2,1)} %tie.62), kind=kOutput, calls=%fused_computation.1 | convolution fusion | flops 4294967296 | bytes 12582912 | tf_op jit(solution)/shard_map/dot_general | solution.py:19
  279.0 42.3 %forward.2 = (f32[4,512,1024]{2,1,0:T(8,128)}, bf16[4,8192,1024]{2,1,0:T(8,128)(2,1)}, bf16[4,512,1024]{2,1,0:T(8,128)(2,1)}, bf16[4,512,1024]{2,1,0:T(8,128)(2,...) custom-call(f32[4,512,1024]{2,1,0:T(8,128)} %get-tuple-element.98.delta_ref, ...), custom_call_target="tpu_custom_call" | custom-call | flops 44999999488 | tf_op jit(solution)/shard_map/forward/pallas_call | solution.py:250
  345.7 41.6 %forward.3 = (f32[4,512,1024]{2,1,0:T(8,128)}, bf16[4,8192,1024]{2,1,0:T(8,128)(2,1)}, bf16[4,512,1024]{2,1,0:T(8,128)(2,1)}, bf16[4,512,1024]{2,1,0:T(8,128)(2,...) custom-call(f32[4,512,1024]{2,1,0:T(8,128)} %get-tuple-element.98.de, ...), custom_call_target="tpu_custom_call", output_to_operand_aliasing={{0}: (10, {}), {1}: (11, {}), {2}: (12, {}), {3}: (13, {}),... | custom-call | flops 44999999488 | tf_op jit(solution)/shard_map/forward/pallas_call | solution.py:250
  412.7 14.0 %convolution_convert_fusion.2.refs_1_ = bf16[2048,1024]{1,0:T(8,128)(2,1)} fusion(bf16[2048,2048]{1,0:T(8,128)(2,1)} %tie.62, bf16[2048,1024]{1,0:T(8,128)(2,1)} %tie.66), kind=kOutput, calls=%fused_computation.8 | convolution fusion | flops 8592031744 | bytes 16777216 | tf_op jit(solution)/shard_map/dot_general | solution.py:27
  426.9 14.0 %convolution_convert_fusion.1.refs_2_ = bf16[2048,1024]{1,0:T(8,128)(2,1)} fusion(bf16[2048,2048]{1,0:T(8,128)(2,1)} %get-tuple-element.92, bf16[2048,1024]{1,0:T(8,128)(2,1)} %bitcast.482), kind=kOutput, calls=%fused_computation.7 | convolution fusion | flops 8592031744 | bytes 16777216 | tf_op jit(solution)/shard_map/dot_general | solution.py:27
  453.3 46.4 %backward.2 = (bf16[4,512,1024]{2,1,0:T(8,128)(2,1)}, f32[4,512,1024]{2,1,0:T(8,128)}, f32[4,32,1,256]{3,2,1,0:T(1,128)}, f32[4,16,1024]{2,1,0:T(8,128)}, f32[4,...) custom-call(f32[4,512,1024]{2,1,0:T(8,128)} %get-tuple-element.110.pre_ref, f32[4,512,1024]{2,1,0:T(8,128)} %get-tuple-element.98.delta_ref, ...), custom_call_target="tpu_custom_call" | custom-call | flops 4000000000 | tf_op jit(solution)/shard_map/backward/pallas_call | solution.py:335
  515.2 46.2 %backward.3 = (bf16[4,512,1024]{2,1,0:T(8,128)(2,1)}, f32[4,512,1024]{2,1,0:T(8,128)}, f32[4,32,1,256]{3,2,1,0:T(1,128)}, f32[4,16,1024]{2,1,0:T(8,128)}, f32[4,...) custom-call(f32[4,512,1024]{2,1,0:T(8,128)} %get-tuple-element.110.pre_ref, ...), custom_call_target="tpu_custom_call", output_to_operand_aliasing={{0}: (11, {}), {1}: (12, {}), {2}: (13, {})} | custom-call | flops 4000000000 | tf_op jit(solution)/shard_map/backward/pallas_call | solution.py:335
  582.9 7.4 fusion.16.refs_1_
  591.7 13.3 %conv_back.2 = (bf16[4,512,1024]{2,1,0:T(8,128)(2,1)}, f32[4,8,1024]{2,1,0:T(8,128)}, f32[4,8,1024]{2,1,0:T(8,128)}, f32[4,40,1024]{2,1,0:T(8,128)}) custom-call(bf16[4,256,160]{2,1,0:T(8,128)(2,1)} %tie.77.dproj_ref, bf16[160,1024]{1,0:T(8,128)(2,1)} %fusion.40.xproj_ref, f32[4,512,1024]{2,1,0:T(8,128)} %get-tuple-element.128.dmix_ref, ...), custom_call_target="tpu_custom_call" | custom-call | flops 200000000 | tf_op jit(solution)/shard_map/conv_back/pallas_call | solution.py:405
  617.4 13.0 %conv_back.3 = (bf16[4,512,1024]{2,1,0:T(8,128)(2,1)}, f32[4,8,1024]{2,1,0:T(8,128)}, f32[4,8,1024]{2,1,0:T(8,128)}, f32[4,40,1024]{2,1,0:T(8,128)}) custom-call(bf16[4,256,160]{2,1,0:T(8,128)(2,1)} %tie.79.dproj_ref, bf16[160,1024]{1,0:T(8,128)(2,1)} %fusion.40.xproj_ref, ...), custom_call_target="tpu_custom_call", output_to_operand_aliasing={{0}: (9, {})} | custom-call | flops 200000000 | tf_op jit(solution)/shard_map/conv_back/pallas_call | solution.py:405
  645.4 14.0 %convolution_convert_fusion.refs_1_ = bf16[2048,1024]{1,0:T(8,128)(2,1)} fusion(bf16[2048,2048]{1,0:T(8,128)(2,1)} %get-tuple-element.92, bf16[2048,1024]{1,0:T(8,128)(2,1)} %bitcast.477), kind=kOutput, calls=%fused_computation.6 | convolution fusion | flops 8592031744 | bytes 16777216 | tf_op jit(solution)/shard_map/dot_general | solution.py:27
  661.4 8.2 %fusion.115 = (bf16[512,2048]{1,0:T(8,128)(2,1)S(1)}, f32[512,2048]{1,0:T(8,128)}) fusion(f32[512,2048]{1,0:T(8,128)} %fusion.16.refs_1_, bf16[2048,1024]{1,0:T(8,128)(2,1)} %all-gather.10.cloned.1.call-done.w_ref, bf16[4,512,1024]{2,1,0:T(8,128)(2,1)} %tie.85.refs_0_.refs_1_), kind=kOutput, calls=%fused_computation.373 | convolution fusion | flops 2149580800 | bytes 15728640 | tf_op jit(solution)/shard_map/dot_general | solution.py:23
  710.4 38.8 %collective-permute-done.47.one_ref.refs_1_ = bf16[512,2048]{1,0:T(8,128)(2,1)} collective-permute-done((bf16[512,2048]{1,0:T(8,128)(2,1)S(1)}, bf16[512,2048]{1,0:T(8,128)(2,1)}, u32[]{:S(2)}, u32[]{:S(2)}) %collective-permute-start.47) | collective-permute-done | bytes 2097184 | tf_op jit(solution)/shard_map/ppermute | solution.py:482
  785.5 7.8 input_gradient.1
  (608 shorter events, 332.9 us)
Async XLA Ops:
  7.2 97.1 %all-gather.10.cloned.1.call-start = ((), (), s32[]{:S(2)}) async-start(), calls=%async_computation.3 | async-start | bytes 4718592 | tf_op jit(solution)/shard_map/all_gather | solution.py:538
  12.4 143.5 %all-gather.12.cloned.1.call-start = ((), (), s32[]{:S(2)}) async-start(), calls=%async_computation.4 | async-start | bytes 4718592 | tf_op jit(solution)/shard_map/all_gather | solution.py:538
  28.5 50.6 %collective-permute-start.8 = (bf16[256,2048]{1,0:T(8,128)(2,1)}, bf16[256,2048]{1,0:T(8,128)(2,1)}, u32[]{:S(2)}, u32[]{:S(2)}) collective-permute-start(bf16[256,2048]{1,0:T(8,128)(2,1)} %tie.46.low_ref), channel_id=1, source_target_pairs={{0,16},{8,24},{16,0},{24,8},{1,17},{9,25},{17,1},{25,9},{2,18},{10... | collective-permute-start | bytes 3145736 | tf_op jit(solution)/shard_map/ppermute | solution.py:482
  29.0 57.1 %collective-permute-start.6 = (bf16[256,2048]{1,0:T(8,128)(2,1)}, bf16[256,2048]{1,0:T(8,128)(2,1)}, u32[]{:S(2)}, u32[]{:S(2)}) collective-permute-start(bf16[256,2048]{1,0:T(8,128)(2,1)} %tie.46.low_ref), channel_id=1, source_target_pairs={{0,8},{8,0},{16,24},{24,16},{1,9},{9,1},{17,25},{25,17},{2,10},{10... | collective-permute-start | bytes 3145736 | tf_op jit(solution)/shard_map/ppermute | solution.py:482
  90.6 142.3 %all-gather.14.cloned.1.call-start = ((), (), s32[]{:S(2)}) async-start(), calls=%async_computation.5 | async-start | bytes 4718592 | tf_op jit(solution)/shard_map/all_gather | solution.py:538
  91.5 167.8 %all-gather.16.cloned.1.call-start = ((), (), s32[]{:S(2)}) async-start(), calls=%async_computation.6 | async-start | bytes 1179648 | tf_op jit(solution)/shard_map/all_gather | solution.py:633
  136.9 55.2 %collective-permute-start.19 = (bf16[256,2048]{1,0:T(8,128)(2,1)}, bf16[256,2048]{1,0:T(8,128)(2,1)S(1)}, u32[]{:S(2)}, u32[]{:S(2)}) collective-permute-start(bf16[256,2048]{1,0:T(8,128)(2,1)} %tie.55), channel_id=1, source_target_pairs={{0,16},{8,24},{16,0},{24,8},{1,17},{9,25},{17,1},{25,9},{2,18},{10... | collective-permute-start | bytes 3145736 | tf_op jit(solution)/shard_map/ppermute | solution.py:482
  138.9 53.1 %collective-permute-start.18 = (bf16[256,2048]{1,0:T(8,128)(2,1)}, bf16[256,2048]{1,0:T(8,128)(2,1)S(1)}, u32[]{:S(2)}, u32[]{:S(2)}) collective-permute-start(bf16[256,2048]{1,0:T(8,128)(2,1)} %tie.55), channel_id=1, source_target_pairs={{0,8},{8,0},{16,24},{24,16},{1,9},{9,1},{17,25},{25,17},{2,10},{10... | collective-permute-start | bytes 3145736 | tf_op jit(solution)/shard_map/ppermute | solution.py:482
  196.0 61.0 %collective-permute-start.21 = (bf16[256,2048]{1,0:T(8,128)(2,1)}, bf16[256,2048]{1,0:T(8,128)(2,1)}, u32[]{:S(2)}, u32[]{:S(2)}) collective-permute-start(bf16[256,2048]{1,0:T(8,128)(2,1)} %tie.57), channel_id=1, source_target_pairs={{0,16},{8,24},{16,0},{24,8},{1,17},{9,25},{17,1},{25,9},{2,18},{10... | collective-permute-start | bytes 3145736 | tf_op jit(solution)/shard_map/ppermute | solution.py:482
  224.7 118.9 %all-gather.18.cloned.1.call-start = ((), (), s32[]{:S(2)}) async-start(), calls=%async_computation.7 | async-start | bytes 1179648 | tf_op jit(solution)/shard_map/all_gather | solution.py:633
  268.9 179.6 %all-gather.20.cloned.1.call-start = ((), (), s32[]{:S(2)}) async-start(), calls=%async_computation.8 | async-start | bytes 1179648 | tf_op jit(solution)/shard_map/all_gather | solution.py:672
  334.6 65.6 %collective-permute-start.24 = (bf16[256,2048]{1,0:T(8,128)(2,1)}, bf16[256,2048]{1,0:T(8,128)(2,1)S(1)}, u32[]{:S(2)}, u32[]{:S(2)}) collective-permute-start(bf16[256,2048]{1,0:T(8,128)(2,1)} %get-tuple-element.152), channel_id=1, source_target_pairs={{0,16},{8,24},{16,0},{24,8},{1,17},{9,25},{17,1},{25,9},{2,18},{10... | collective-permute-start | bytes 3145736 | tf_op jit(solution)/shard_map/ppermute | solution.py:482
  335.5 61.6 %collective-permute-start.26 = (bf16[256,2048]{1,0:T(8,128)(2,1)}, bf16[256,2048]{1,0:T(8,128)(2,1)S(1)}, u32[]{:S(2)}, u32[]{:S(2)}) collective-permute-start(bf16[256,2048]{1,0:T(8,128)(2,1)} %get-tuple-element.153), channel_id=1, source_target_pairs={{0,8},{8,0},{16,24},{24,16},{1,9},{9,1},{17,25},{25,17},{2,10},{10... | collective-permute-start | bytes 3145736 | tf_op jit(solution)/shard_map/ppermute | solution.py:482
  388.9 110.8 %reduce-scatter.4.cloned.1.call-start = ((), (), s32[]{:S(2)}) async-start(), calls=%async_computation.9 | async-start | bytes 4718592 | tf_op jit(solution)/shard_map/reduce_scatter | solution.py:680
  426.7 143.2 %reduce-scatter.6.cloned.1.call-start = ((), (), s32[]{:S(2)}) async-start(), calls=%async_computation.11 | async-start | bytes 4718592 | tf_op jit(solution)/shard_map/reduce_scatter | solution.py:680
  441.0 134.1 %all-gather.22.cloned.1.call-start = ((), (), s32[]{:S(2)}) async-start(), calls=%async_computation.10 | async-start | bytes 2621440 | tf_op jit(solution)/shard_map/all_gather | solution.py:683
  445.3 60.1 %collective-permute-start.27 = (bf16[512,2048]{1,0:T(8,128)(2,1)}, bf16[512,2048]{1,0:T(8,128)(2,1)S(1)}, u32[]{:S(2)}, u32[]{:S(2)}) collective-permute-start(bf16[512,2048]{1,0:T(8,128)(2,1)} %pad_maximum_fusion.1.refs_2_), channel_id=1, source_target_pairs={{0,16},{8,24},{16,0},{24,8},{1,17},{9,25},{17,1},{25,9},{2,18},{10... | collective-permute-start | bytes 6291464 | tf_op jit(solution)/shard_map/ppermute | solution.py:482
  446.0 59.4 %collective-permute-start.25 = (bf16[512,2048]{1,0:T(8,128)(2,1)}, bf16[512,2048]{1,0:T(8,128)(2,1)}, u32[]{:S(2)}, u32[]{:S(2)}) collective-permute-start(bf16[512,2048]{1,0:T(8,128)(2,1)} %pad_maximum_fusion.refs_1_), channel_id=1, source_target_pairs={{0,8},{8,0},{16,24},{24,16},{1,9},{9,1},{17,25},{25,17},{2,10},{10... | collective-permute-start | bytes 6291464 | tf_op jit(solution)/shard_map/ppermute | solution.py:482
  499.8 117.6 %all-gather.24.cloned.1.call-start = ((), (), s32[]{:S(2)}) async-start(), calls=%async_computation.12 | async-start | bytes 2621440 | tf_op jit(solution)/shard_map/all_gather | solution.py:683
  510.8 52.0 %collective-permute-start.30 = (bf16[256,160]{1,0:T(8,128)(2,1)S(1)}, bf16[256,160]{1,0:T(8,128)(2,1)S(1)}, u32[]{:S(2)}, u32[]{:S(2)}) collective-permute-start(bf16[256,160]{1,0:T(8,128)(2,1)S(1)} %get-tuple-element.177.refs_3_), channel_id=1, source_target_pairs={{0,24},{8,16},{16,8},{24,0},{1,25},{9,17},{17,9},{25,1},{2,26},{10... | collective-permute-start | bytes 245768 | tf_op jit(solution)/shard_map/ppermute | solution.py:482
  512.2 51.3 %collective-permute-start.29 = (bf16[256,160]{1,0:T(8,128)(2,1)S(1)}, bf16[256,160]{1,0:T(8,128)(2,1)S(1)}, u32[]{:S(2)}, u32[]{:S(2)}) collective-permute-start(bf16[256,160]{1,0:T(8,128)(2,1)S(1)} %get-tuple-element.178.refs_2_), channel_id=1, source_target_pairs={{0,16},{8,24},{16,0},{24,8},{1,17},{9,25},{17,1},{25,9},{2,18},{10... | collective-permute-start | bytes 245768 | tf_op jit(solution)/shard_map/ppermute | solution.py:482
  513.7 50.4 %collective-permute-start.28 = (bf16[256,160]{1,0:T(8,128)(2,1)S(1)}, bf16[256,160]{1,0:T(8,128)(2,1)S(1)}, u32[]{:S(2)}, u32[]{:S(2)}) collective-permute-start(bf16[256,160]{1,0:T(8,128)(2,1)S(1)} %copy-done.68), channel_id=1, source_target_pairs={{0,8},{8,0},{16,24},{24,16},{1,9},{9,1},{17,25},{25,17},{2,10},{10... | collective-permute-start | bytes 245768 | tf_op jit(solution)/shard_map/ppermute | solution.py:482
  570.0 184.6 %reduce-scatter.8.cloned.1.call-start = ((), (), s32[]{:S(2)}) async-start(), calls=%async_computation.13 | async-start | bytes 4718592 | tf_op jit(solution)/shard_map/reduce_scatter | solution.py:680
  706.5 48.1 %collective-permute-start.49 = (bf16[512,2048]{1,0:T(8,128)(2,1)}, bf16[512,2048]{1,0:T(8,128)(2,1)}, u32[]{:S(2)}, u32[]{:S(2)}) collective-permute-start(bf16[512,2048]{1,0:T(8,128)(2,1)} %pad_maximum_fusion.3.refs_2_), channel_id=1, source_target_pairs={{0,16},{8,24},{16,0},{24,8},{1,17},{9,25},{17,1},{25,9},{2,18},{10... | collective-permute-start | bytes 6291464 | tf_op jit(solution)/shard_map/ppermute | solution.py:482
  (155 other events, 2045.0 us)
Sparse Core Ops, SparseCore 0:
  12.5 70.5 all-gather.9
  90.7 46.6 all-gather.11
  138.9 45.8 all-gather.13
  224.8 20.7 all-gather.15
  269.1 20.5 all-gather.17
  389.0 20.7 all-gather.19
  426.8 48.5 reduce-scatter.3
  477.7 48.1 reduce-scatter.5
  527.7 33.4 all-gather.21
  570.1 39.3 all-gather.23
  659.5 50.4 reduce-scatter.7
  757.0 36.7 all-gather.25

commit v3 on v2

--- a/solution.py
+++ b/solution.py
@@ -94,7 +94,7 @@
     xs_ref[:8] = xs_ref[step:step + 8]
 
 
-def front(slot, docs, kept, first, top, low, halo, w, small, lead, cols, init, step=128):
+def front(slot, docs, kept, first, top, low, halo, w, small, lead, cols, init, step=256):
     width, block = w.shape
     extra = 16
     tokens = 2 * top.shape[0]

time: 815 us -> 814 us (level)
  no operation moved by 1% of the time
where the time goes in v3:
time: 814 us; the launch traced here: 808 us
  Pallas kernels  303 us (37%)
  matrix products  137 us (17%)
  waiting for transfers between devices  129 us (16%)
  local copies, waits for them, and re-layouts  81.9 us (10%)
  other arithmetic  72.8 us (9%)
  starting transfers between devices  68.5 us (8%)
  between operations  16.5 us (2%)
    ppermute x49, waiting for transfers between devices, swap(): lax.ppermute(x, axis, [(i, i ^ flip) for i in range(lax.axis_size(axis))])  126 us
    pallas_call x2, Pallas kernels, backward(): pl.pallas_call(backward_kernel, out_shape=[shape(delta.shape, BF), shape(...  92.6 us
    pallas_call x2, Pallas kernels, forward(): pl.pallas_call(forward_kernel, out_shape=[shape(delta.shape), shape((docs...  83.4 us
    dot_general x14, matrix products, mm_last(): return lax.dot_general(a, b, LAST, preferred_element_type=F32)  59.5 us
    ppermute x49, starting transfers between devices, swap(): lax.ppermute(x, axis, [(i, i ^ flip) for i in range(lax.axis_size(axis))])  56.3 us
    pallas_call x2, Pallas kernels, summary(): pl.pallas_call(summary_kernel, out_shape=[shape((docs, tokens, width))] *...  44.1 us
    dot_general x5, matrix products, mm_first(): return lax.dot_general(a, b, FIRST, preferred_element_type=F32)  43.5 us
    pallas_call x4, Pallas kernels, front(): pl.pallas_call(functools.partial(front_kernel, lead=lead), out_shape=[sha...  38.3 us
  transfers between devices with their start and end apart: 68, of which 19 were waited for; matrix products, arithmetic and copies ran while one was open for 31% of the time, Pallas kernels for 37%

profile of v3, /device:TPU:0, one launch (start us, length us, event | category | flops | bytes accessed | tf_op | source)
XLA Modules:
  0.0 808.0 jit_solution(16186254323089621643)
XLA Ops:
  35.0 16.6 %collective-permute-done.7.refs_3_.top_ref = bf16[256,2048]{1,0:T(8,128)(2,1)} collective-permute-done((bf16[256,2048]{1,0:T(8,128)(2,1)}, bf16[256,2048]{1,0:T(8,128)(2,1)}, u32[]{:S(2)}, u32[]{:S(2)}) %collective-permute-start.7) | collective-permute-done | bytes 1048608 | tf_op jit(solution)/shard_map/ppermute | solution.py:482
  51.6 10.4 %collective-permute-done.5.refs_1_.top_ref = bf16[256,2048]{1,0:T(8,128)(2,1)S(1)} collective-permute-done((bf16[256,2048]{1,0:T(8,128)(2,1)}, bf16[256,2048]{1,0:T(8,128)(2,1)S(1)}, u32[]{:S(2)}, u32[]{:S(2)}) %collective-permute-start.5) | collective-permute-done | bytes 1048608 | tf_op jit(solution)/shard_map/ppermute | solution.py:482
  62.0 17.2 %collective-permute-done.8.refs_4_.low_ref = bf16[256,2048]{1,0:T(8,128)(2,1)} collective-permute-done((bf16[256,2048]{1,0:T(8,128)(2,1)}, bf16[256,2048]{1,0:T(8,128)(2,1)}, u32[]{:S(2)}, u32[]{:S(2)}) %collective-permute-start.8) | collective-permute-done | bytes 1048608 | tf_op jit(solution)/shard_map/ppermute | solution.py:482
  104.1 9.7 %front.4 = (bf16[2048,2048]{1,0:T(8,128)(2,1)}, f32[4,512,1024]{2,1,0:T(8,128)}, bf16[4,512,1024]{2,1,0:T(8,128)(2,1)}, f32[4,8,1024]{2,1,0:T(8,128)}, f32[512,160]{1,0:T(8,128)}) custom-call(s32[1]{0:T(128)} %bitcast.1.first_ref, bf16[256,2048]{1,0:T(8,128)(2,1)} %get-tuple-element.157.top_ref, bf16[256,2048]{1,0:T(8,128)(2,1)} %tie.46.low_ref, ...), custom_call_target="tpu_custom_call" | custom-call | flops 100000000 | tf_op jit(solution)/shard_map/front/pallas_call | solution.py:104
  113.9 9.5 %front.5 = (bf16[2048,2048]{1,0:T(8,128)(2,1)}, f32[4,512,1024]{2,1,0:T(8,128)}, bf16[4,512,1024]{2,1,0:T(8,128)(2,1)}, f32[4,8,1024]{2,1,0:T(8,128)}, f32[512,160]{1,0:T(8,128)}) custom-call(s32[1]{0:T(128)} %bitcast.1.first_ref, bf16[256,2048]{1,0:T(8,128)(2,1)} %copy-done.32, ...), custom_call_target="tpu_custom_call", output_to_operand_aliasing={{0}: (8, {}), {1}: (9, {}), {2}: (10, {}), {3}: (11, {})} | custom-call | flops 100000000 | tf_op jit(solution)/shard_map/front/pallas_call | solution.py:104
  123.4 9.5 %front.6 = (bf16[2048,2048]{1,0:T(8,128)(2,1)}, f32[4,512,1024]{2,1,0:T(8,128)}, bf16[4,512,1024]{2,1,0:T(8,128)(2,1)}, f32[4,8,1024]{2,1,0:T(8,128)}, f32[512,160]{1,0:T(8,128)}) custom-call(s32[1]{0:T(128)} %bitcast.1.first_ref, ...), custom_call_target="tpu_custom_call", output_to_operand_aliasing={{0}: (8, {}), {1}: (9, {}), {2}: (10, {}), {3}: (11, {})} | custom-call | flops 100000000 | tf_op jit(solution)/shard_map/front/pallas_call | solution.py:104
  136.9 9.5 %front.7 = (bf16[2048,2048]{1,0:T(8,128)(2,1)}, f32[4,512,1024]{2,1,0:T(8,128)}, bf16[4,512,1024]{2,1,0:T(8,128)(2,1)}, f32[4,8,1024]{2,1,0:T(8,128)}, f32[512,160]{1,0:T(8,128)}) custom-call(s32[1]{0:T(128)} %bitcast.1.first_ref, bf16[256,2048]{1,0:T(8,128)(2,1)} %tie.48.top_ref.refs_1_, ...), custom_call_target="tpu_custom_call", output_to_operand_aliasing={{0}: (8, {}), {1}: (9, {}), {2}: (10, {}), {3}: (11, {})} | custom-call | flops 100000000 | tf_op jit(solution)/shard_map/front/pallas_call | solution.py:104
  153.1 14.9 %fusion.116.refs_1_ = f32[2048,1024]{1,0:T(8,128)} fusion(bf16[2048,2048]{1,0:T(8,128)(2,1)} %get-tuple-element.92, bf16[2048,1024]{1,0:T(8,128)(2,1)} %tie.51), kind=kOutput, calls=%fused_computation.374 | convolution fusion | flops 8589934592 | bytes 20971520 | tf_op jit(solution)/shard_map/dot_general | solution.py:19
  198.9 22.1 %summary.2 = (f32[4,512,1024]{2,1,0:T(8,128)}, f32[4,512,1024]{2,1,0:T(8,128)}, f32[2,16,1024]{2,1,0:T(8,128)}, f32[2,16,1024]{2,1,0:T(8,128)}) custom-call(bf16[4,512,128]{2,1,0:T(8,128)(2,1)} %bitcast.510, bf16[128,1024]{1,0:T(8,128)(2,1)} %fusion.48.dtw_ref, f32[1,1024]{1,0:T(1,128)} %get-tuple-element.163.shift_ref, ...), custom_call_target="tpu_custom_call" | custom-call | flops 22000001024 | tf_op jit(solution)/shard_map/summary/pallas_call | solution.py:165
  232.0 22.0 %summary.3 = (f32[4,512,1024]{2,1,0:T(8,128)}, f32[4,512,1024]{2,1,0:T(8,128)}, f32[2,16,1024]{2,1,0:T(8,128)}, f32[2,16,1024]{2,1,0:T(8,128)}) custom-call(bf16[4,512,128]{2,1,0:T(8,128)(2,1)} %bitcast.511, bf16[128,1024]{1,0:T(8,128)(2,1)} %fusion.48.dtw_ref, ...), custom_call_target="tpu_custom_call", output_to_operand_aliasing={{0}: (6, {}), {1}: (7, {})} | custom-call | flops 22000001024 | tf_op jit(solution)/shard_map/summary/pallas_call | solution.py:165
  267.1 10.0 %fusion = f32[1024,1024]{1,0:T(8,128)} fusion(bf16[2048,1024]{1,0:T(8,128)(2,1)} %all-gather.14.cloned.1.call-done.refs_2_, bf16[2048,2048]{1,0:T(8,128)(2,1)} %tie.62), kind=kOutput, calls=%fused_computation.1 | convolution fusion | flops 4294967296 | bytes 12582912 | tf_op jit(solution)/shard_map/dot_general | solution.py:19
  277.1 41.8 %forward.2 = (f32[4,512,1024]{2,1,0:T(8,128)}, bf16[4,8192,1024]{2,1,0:T(8,128)(2,1)}, bf16[4,512,1024]{2,1,0:T(8,128)(2,1)}, bf16[4,512,1024]{2,1,0:T(8,128)(2,...) custom-call(f32[4,512,1024]{2,1,0:T(8,128)} %get-tuple-element.98.delta_ref, ...), custom_call_target="tpu_custom_call" | custom-call | flops 44999999488 | tf_op jit(solution)/shard_map/forward/pallas_call | solution.py:250
  343.4 41.6 %forward.3 = (f32[4,512,1024]{2,1,0:T(8,128)}, bf16[4,8192,1024]{2,1,0:T(8,128)(2,1)}, bf16[4,512,1024]{2,1,0:T(8,128)(2,1)}, bf16[4,512,1024]{2,1,0:T(8,128)(2,...) custom-call(f32[4,512,1024]{2,1,0:T(8,128)} %get-tuple-element.98.de, ...), custom_call_target="tpu_custom_call", output_to_operand_aliasing={{0}: (10, {}), {1}: (11, {}), {2}: (12, {}), {3}: (13, {}),... | custom-call | flops 44999999488 | tf_op jit(solution)/shard_map/forward/pallas_call | solution.py:250
  410.4 14.0 %convolution_convert_fusion.2.refs_1_ = bf16[2048,1024]{1,0:T(8,128)(2,1)} fusion(bf16[2048,2048]{1,0:T(8,128)(2,1)} %tie.62, bf16[2048,1024]{1,0:T(8,128)(2,1)} %tie.66), kind=kOutput, calls=%fused_computation.8 | convolution fusion | flops 8592031744 | bytes 16777216 | tf_op jit(solution)/shard_map/dot_general | solution.py:27
  424.9 14.0 %convolution_convert_fusion.1.refs_2_ = bf16[2048,1024]{1,0:T(8,128)(2,1)} fusion(bf16[2048,2048]{1,0:T(8,128)(2,1)} %get-tuple-element.92, bf16[2048,1024]{1,0:T(8,128)(2,1)} %bitcast.482), kind=kOutput, calls=%fused_computation.7 | convolution fusion | flops 8592031744 | bytes 16777216 | tf_op jit(solution)/shard_map/dot_general | solution.py:27
  451.2 46.4 %backward.2 = (bf16[4,512,1024]{2,1,0:T(8,128)(2,1)}, f32[4,512,1024]{2,1,0:T(8,128)}, f32[4,32,1,256]{3,2,1,0:T(1,128)}, f32[4,16,1024]{2,1,0:T(8,128)}, f32[4,...) custom-call(f32[4,512,1024]{2,1,0:T(8,128)} %get-tuple-element.110.pre_ref, f32[4,512,1024]{2,1,0:T(8,128)} %get-tuple-element.98.delta_ref, ...), custom_call_target="tpu_custom_call" | custom-call | flops 4000000000 | tf_op jit(solution)/shard_map/backward/pallas_call | solution.py:335
  513.1 46.2 %backward.3 = (bf16[4,512,1024]{2,1,0:T(8,128)(2,1)}, f32[4,512,1024]{2,1,0:T(8,128)}, f32[4,32,1,256]{3,2,1,0:T(1,128)}, f32[4,16,1024]{2,1,0:T(8,128)}, f32[4,...) custom-call(f32[4,512,1024]{2,1,0:T(8,128)} %get-tuple-element.110.pre_ref, ...), custom_call_target="tpu_custom_call", output_to_operand_aliasing={{0}: (11, {}), {1}: (12, {}), {2}: (13, {})} | custom-call | flops 4000000000 | tf_op jit(solution)/shard_map/backward/pallas_call | solution.py:335
  580.7 7.3 fusion.16.refs_1_
  589.5 13.4 %conv_back.2 = (bf16[4,512,1024]{2,1,0:T(8,128)(2,1)}, f32[4,8,1024]{2,1,0:T(8,128)}, f32[4,8,1024]{2,1,0:T(8,128)}, f32[4,40,1024]{2,1,0:T(8,128)}) custom-call(bf16[4,256,160]{2,1,0:T(8,128)(2,1)} %tie.77.dproj_ref, bf16[160,1024]{1,0:T(8,128)(2,1)} %fusion.40.xproj_ref, f32[4,512,1024]{2,1,0:T(8,128)} %get-tuple-element.128.dmix_ref, ...), custom_call_target="tpu_custom_call" | custom-call | flops 200000000 | tf_op jit(solution)/shard_map/conv_back/pallas_call | solution.py:405
  615.2 13.0 %conv_back.3 = (bf16[4,512,1024]{2,1,0:T(8,128)(2,1)}, f32[4,8,1024]{2,1,0:T(8,128)}, f32[4,8,1024]{2,1,0:T(8,128)}, f32[4,40,1024]{2,1,0:T(8,128)}) custom-call(bf16[4,256,160]{2,1,0:T(8,128)(2,1)} %tie.79.dproj_ref, bf16[160,1024]{1,0:T(8,128)(2,1)} %fusion.40.xproj_ref, ...), custom_call_target="tpu_custom_call", output_to_operand_aliasing={{0}: (9, {})} | custom-call | flops 200000000 | tf_op jit(solution)/shard_map/conv_back/pallas_call | solution.py:405
  643.3 14.0 %convolution_convert_fusion.refs_1_ = bf16[2048,1024]{1,0:T(8,128)(2,1)} fusion(bf16[2048,2048]{1,0:T(8,128)(2,1)} %get-tuple-element.92, bf16[2048,1024]{1,0:T(8,128)(2,1)} %bitcast.477), kind=kOutput, calls=%fused_computation.6 | convolution fusion | flops 8592031744 | bytes 16777216 | tf_op jit(solution)/shard_map/dot_general | solution.py:27
  659.3 8.2 %fusion.115 = (bf16[512,2048]{1,0:T(8,128)(2,1)S(1)}, f32[512,2048]{1,0:T(8,128)}) fusion(f32[512,2048]{1,0:T(8,128)} %fusion.16.refs_1_, bf16[2048,1024]{1,0:T(8,128)(2,1)} %all-gather.10.cloned.1.call-done.w_ref, bf16[4,512,1024]{2,1,0:T(8,128)(2,1)} %tie.85.refs_0_.refs_1_), kind=kOutput, calls=%fused_computation.373 | convolution fusion | flops 2149580800 | bytes 15728640 | tf_op jit(solution)/shard_map/dot_general | solution.py:23
  708.4 38.7 %collective-permute-done.47.one_ref.refs_1_ = bf16[512,2048]{1,0:T(8,128)(2,1)} collective-permute-done((bf16[512,2048]{1,0:T(8,128)(2,1)S(1)}, bf16[512,2048]{1,0:T(8,128)(2,1)}, u32[]{:S(2)}, u32[]{:S(2)}) %collective-permute-start.47) | collective-permute-done | bytes 2097184 | tf_op jit(solution)/shard_map/ppermute | solution.py:482
  783.4 7.8 input_gradient.1
  (608 shorter events, 333.6 us)
Async XLA Ops:
  7.2 96.9 %all-gather.10.cloned.1.call-start = ((), (), s32[]{:S(2)}) async-start(), calls=%async_computation.3 | async-start | bytes 4718592 | tf_op jit(solution)/shard_map/all_gather | solution.py:538
  12.4 140.7 %all-gather.12.cloned.1.call-start = ((), (), s32[]{:S(2)}) async-start(), calls=%async_computation.4 | async-start | bytes 4718592 | tf_op jit(solution)/shard_map/all_gather | solution.py:538
  28.5 50.6 %collective-permute-start.8 = (bf16[256,2048]{1,0:T(8,128)(2,1)}, bf16[256,2048]{1,0:T(8,128)(2,1)}, u32[]{:S(2)}, u32[]{:S(2)}) collective-permute-start(bf16[256,2048]{1,0:T(8,128)(2,1)} %tie.46.low_ref), channel_id=1, source_target_pairs={{0,16},{8,24},{16,0},{24,8},{1,17},{9,25},{17,1},{25,9},{2,18},{10... | collective-permute-start | bytes 3145736 | tf_op jit(solution)/shard_map/ppermute | solution.py:482
  29.0 57.1 %collective-permute-start.6 = (bf16[256,2048]{1,0:T(8,128)(2,1)}, bf16[256,2048]{1,0:T(8,128)(2,1)}, u32[]{:S(2)}, u32[]{:S(2)}) collective-permute-start(bf16[256,2048]{1,0:T(8,128)(2,1)} %tie.46.low_ref), channel_id=1, source_target_pairs={{0,8},{8,0},{16,24},{24,16},{1,9},{9,1},{17,25},{25,17},{2,10},{10... | collective-permute-start | bytes 3145736 | tf_op jit(solution)/shard_map/ppermute | solution.py:482
  90.6 140.3 %all-gather.14.cloned.1.call-start = ((), (), s32[]{:S(2)}) async-start(), calls=%async_computation.5 | async-start | bytes 4718592 | tf_op jit(solution)/shard_map/all_gather | solution.py:538
  91.5 165.8 %all-gather.16.cloned.1.call-start = ((), (), s32[]{:S(2)}) async-start(), calls=%async_computation.6 | async-start | bytes 1179648 | tf_op jit(solution)/shard_map/all_gather | solution.py:633
  134.9 55.2 %collective-permute-start.19 = (bf16[256,2048]{1,0:T(8,128)(2,1)}, bf16[256,2048]{1,0:T(8,128)(2,1)S(1)}, u32[]{:S(2)}, u32[]{:S(2)}) collective-permute-start(bf16[256,2048]{1,0:T(8,128)(2,1)} %tie.55), channel_id=1, source_target_pairs={{0,16},{8,24},{16,0},{24,8},{1,17},{9,25},{17,1},{25,9},{2,18},{10... | collective-permute-start | bytes 3145736 | tf_op jit(solution)/shard_map/ppermute | solution.py:482
  136.9 53.2 %collective-permute-start.18 = (bf16[256,2048]{1,0:T(8,128)(2,1)}, bf16[256,2048]{1,0:T(8,128)(2,1)S(1)}, u32[]{:S(2)}, u32[]{:S(2)}) collective-permute-start(bf16[256,2048]{1,0:T(8,128)(2,1)} %tie.55), channel_id=1, source_target_pairs={{0,8},{8,0},{16,24},{24,16},{1,9},{9,1},{17,25},{25,17},{2,10},{10... | collective-permute-start | bytes 3145736 | tf_op jit(solution)/shard_map/ppermute | solution.py:482
  193.9 61.0 %collective-permute-start.21 = (bf16[256,2048]{1,0:T(8,128)(2,1)}, bf16[256,2048]{1,0:T(8,128)(2,1)}, u32[]{:S(2)}, u32[]{:S(2)}) collective-permute-start(bf16[256,2048]{1,0:T(8,128)(2,1)} %tie.57), channel_id=1, source_target_pairs={{0,16},{8,24},{16,0},{24,8},{1,17},{9,25},{17,1},{25,9},{2,18},{10... | collective-permute-start | bytes 3145736 | tf_op jit(solution)/shard_map/ppermute | solution.py:482
  222.7 118.6 %all-gather.18.cloned.1.call-start = ((), (), s32[]{:S(2)}) async-start(), calls=%async_computation.7 | async-start | bytes 1179648 | tf_op jit(solution)/shard_map/all_gather | solution.py:633
  266.9 179.5 %all-gather.20.cloned.1.call-start = ((), (), s32[]{:S(2)}) async-start(), calls=%async_computation.8 | async-start | bytes 1179648 | tf_op jit(solution)/shard_map/all_gather | solution.py:672
  332.3 65.7 %collective-permute-start.24 = (bf16[256,2048]{1,0:T(8,128)(2,1)}, bf16[256,2048]{1,0:T(8,128)(2,1)S(1)}, u32[]{:S(2)}, u32[]{:S(2)}) collective-permute-start(bf16[256,2048]{1,0:T(8,128)(2,1)} %get-tuple-element.152), channel_id=1, source_target_pairs={{0,16},{8,24},{16,0},{24,8},{1,17},{9,25},{17,1},{25,9},{2,18},{10... | collective-permute-start | bytes 3145736 | tf_op jit(solution)/shard_map/ppermute | solution.py:482
  333.1 61.7 %collective-permute-start.26 = (bf16[256,2048]{1,0:T(8,128)(2,1)}, bf16[256,2048]{1,0:T(8,128)(2,1)S(1)}, u32[]{:S(2)}, u32[]{:S(2)}) collective-permute-start(bf16[256,2048]{1,0:T(8,128)(2,1)} %get-tuple-element.153), channel_id=1, source_target_pairs={{0,8},{8,0},{16,24},{24,16},{1,9},{9,1},{17,25},{25,17},{2,10},{10... | collective-permute-start | bytes 3145736 | tf_op jit(solution)/shard_map/ppermute | solution.py:482
  386.6 111.0 %reduce-scatter.4.cloned.1.call-start = ((), (), s32[]{:S(2)}) async-start(), calls=%async_computation.9 | async-start | bytes 4718592 | tf_op jit(solution)/shard_map/reduce_scatter | solution.py:680
  424.4 143.2 %reduce-scatter.6.cloned.1.call-start = ((), (), s32[]{:S(2)}) async-start(), calls=%async_computation.11 | async-start | bytes 4718592 | tf_op jit(solution)/shard_map/reduce_scatter | solution.py:680
  438.9 134.0 %all-gather.22.cloned.1.call-start = ((), (), s32[]{:S(2)}) async-start(), calls=%async_computation.10 | async-start | bytes 2621440 | tf_op jit(solution)/shard_map/all_gather | solution.py:683
  443.2 60.0 %collective-permute-start.27 = (bf16[512,2048]{1,0:T(8,128)(2,1)}, bf16[512,2048]{1,0:T(8,128)(2,1)S(1)}, u32[]{:S(2)}, u32[]{:S(2)}) collective-permute-start(bf16[512,2048]{1,0:T(8,128)(2,1)} %pad_maximum_fusion.1.refs_2_), channel_id=1, source_target_pairs={{0,16},{8,24},{16,0},{24,8},{1,17},{9,25},{17,1},{25,9},{2,18},{10... | collective-permute-start | bytes 6291464 | tf_op jit(solution)/shard_map/ppermute | solution.py:482
  443.8 59.4 %collective-permute-start.25 = (bf16[512,2048]{1,0:T(8,128)(2,1)}, bf16[512,2048]{1,0:T(8,128)(2,1)}, u32[]{:S(2)}, u32[]{:S(2)}) collective-permute-start(bf16[512,2048]{1,0:T(8,128)(2,1)} %pad_maximum_fusion.refs_1_), channel_id=1, source_target_pairs={{0,8},{8,0},{16,24},{24,16},{1,9},{9,1},{17,25},{25,17},{2,10},{10... | collective-permute-start | bytes 6291464 | tf_op jit(solution)/shard_map/ppermute | solution.py:482
  497.6 117.6 %all-gather.24.cloned.1.call-start = ((), (), s32[]{:S(2)}) async-start(), calls=%async_computation.12 | async-start | bytes 2621440 | tf_op jit(solution)/shard_map/all_gather | solution.py:683
  508.7 52.0 %collective-permute-start.30 = (bf16[256,160]{1,0:T(8,128)(2,1)S(1)}, bf16[256,160]{1,0:T(8,128)(2,1)S(1)}, u32[]{:S(2)}, u32[]{:S(2)}) collective-permute-start(bf16[256,160]{1,0:T(8,128)(2,1)S(1)} %get-tuple-element.177.refs_3_), channel_id=1, source_target_pairs={{0,24},{8,16},{16,8},{24,0},{1,25},{9,17},{17,9},{25,1},{2,26},{10... | collective-permute-start | bytes 245768 | tf_op jit(solution)/shard_map/ppermute | solution.py:482
  510.2 51.2 %collective-permute-start.29 = (bf16[256,160]{1,0:T(8,128)(2,1)S(1)}, bf16[256,160]{1,0:T(8,128)(2,1)S(1)}, u32[]{:S(2)}, u32[]{:S(2)}) collective-permute-start(bf16[256,160]{1,0:T(8,128)(2,1)S(1)} %get-tuple-element.178.refs_2_), channel_id=1, source_target_pairs={{0,16},{8,24},{16,0},{24,8},{1,17},{9,25},{17,1},{25,9},{2,18},{10... | collective-permute-start | bytes 245768 | tf_op jit(solution)/shard_map/ppermute | solution.py:482
  511.6 50.3 %collective-permute-start.28 = (bf16[256,160]{1,0:T(8,128)(2,1)S(1)}, bf16[256,160]{1,0:T(8,128)(2,1)S(1)}, u32[]{:S(2)}, u32[]{:S(2)}) collective-permute-start(bf16[256,160]{1,0:T(8,128)(2,1)S(1)} %copy-done.68), channel_id=1, source_target_pairs={{0,8},{8,0},{16,24},{24,16},{1,9},{9,1},{17,25},{25,17},{2,10},{10... | collective-permute-start | bytes 245768 | tf_op jit(solution)/shard_map/ppermute | solution.py:482
  567.9 184.7 %reduce-scatter.8.cloned.1.call-start = ((), (), s32[]{:S(2)}) async-start(), calls=%async_computation.13 | async-start | bytes 4718592 | tf_op jit(solution)/shard_map/reduce_scatter | solution.py:680
  704.4 48.2 %collective-permute-start.49 = (bf16[512,2048]{1,0:T(8,128)(2,1)}, bf16[512,2048]{1,0:T(8,128)(2,1)}, u32[]{:S(2)}, u32[]{:S(2)}) collective-permute-start(bf16[512,2048]{1,0:T(8,128)(2,1)} %pad_maximum_fusion.3.refs_2_), channel_id=1, source_target_pairs={{0,16},{8,24},{16,0},{24,8},{1,17},{9,25},{17,1},{25,9},{2,18},{10... | collective-permute-start | bytes 6291464 | tf_op jit(solution)/shard_map/ppermute | solution.py:482
  (155 other events, 2036.4 us)
Sparse Core Ops, SparseCore 0:
  12.5 70.5 all-gather.9
  90.7 46.6 all-gather.11
  138.9 45.8 all-gather.13
  222.8 20.5 all-gather.15
  267.0 20.6 all-gather.17
  386.7 20.5 all-gather.19
  424.6 48.4 reduce-scatter.3
  475.4 48.1 reduce-scatter.5
  525.4 33.4 all-gather.21
  568.0 39.0 all-gather.23
  657.4 50.2 reduce-scatter.7
  754.9 36.6 all-gather.25
